TPU v7x, 32 devices: a whole 2x2x4 slice. The times are simulated.
32 devices in a mesh: ctx: 8 (over z, x), wsh: 4 (over y, core).
Axes of the slice: x: 2, y: 2, z: 4, core: 2. Of those that a mesh axis runs over, the one named last changes fastest.
Arguments:
- block_in: bfloat16 [4, 1024, 1088], P('wsh', 'ctx'), may hold values from -6 to 6
- doc_flags: int32 [4, 1024], P('wsh', 'ctx'), may hold values from 0 to 1, as said below
- ln1_gain: bfloat16 [1088], P('wsh'), may hold values from 0.5 to 1.5
- ln1_bias: bfloat16 [1088], P('wsh'), may hold values from -1 to 1
- w_qkv: bfloat16 [1088, 3264], P('wsh'), may hold values from -0.1875 to 0.1875
- qv_bias: bfloat16 [2176], P('wsh'), may hold values from -1 to 1
- w_out: bfloat16 [1088, 1088], P('wsh'), may hold values from -2 to 2
- out_bias: bfloat16 [1088], P('wsh'), may hold values from -1 to 1
- ln2_gain: bfloat16 [1088], P('wsh'), may hold values from 0.5 to 1.5
- ln2_bias: bfloat16 [1088], P('wsh'), may hold values from -1 to 1
- w_up: bfloat16 [1088, 4352], P(None, 'wsh'), may hold values from -0.1875 to 0.1875
- up_bias: bfloat16 [4352], P('wsh'), may hold values from -1 to 1
- w_down: bfloat16 [4352, 1088], P('wsh'), may hold values from -0.09375 to 0.09375
- down_bias: bfloat16 [1088], P('wsh'), may hold values from -1 to 1
- cotangent: bfloat16 [4, 1024, 1088], P('wsh', 'ctx'), may hold values from -6 to 6
Outputs:
- block_out: bfloat16 [4, 1024, 1088], P('wsh', 'ctx')
- input_grad: bfloat16 [4, 1024, 1088], P('wsh', 'ctx')
- grad_ln1_gain: float32 [1088], P('wsh')
- grad_ln1_bias: float32 [1088], P('wsh')
- grad_w_qkv: float32 [1088, 3264], P('wsh')
- grad_qv_bias: float32 [2176], P('wsh')
- grad_w_out: float32 [1088, 1088], P('wsh')
- grad_out_bias: float32 [1088], P('wsh')
- grad_ln2_gain: float32 [1088], P('wsh')
- grad_ln2_bias: float32 [1088], P('wsh')
- grad_w_up: float32 [1088, 4352], P(None, 'wsh')
- grad_up_bias: float32 [4352], P('wsh')
- grad_w_down: float32 [4352, 1088], P('wsh')
- grad_down_bias: float32 [1088], P('wsh')
- rms_values: float32 [4, 3], P('wsh')
Inputs may be any that keep to these rules, and one draw needn't show every extreme that they name: `doc_flags`: each stream has a 1 at position 0. In one stream, one document starts within the first 128 positions and ends within the last 128, and every other document of that stream lies inside those two ranges. In every other stream no document has more than 256 tokens, and one has exactly 256.
All inputs are finite; a program needn't handle non-finite values.
Results may differ from a plain program's by a relative error of at most 0.03.
Values may be sent and summed in bfloat16 or wider, within the bound.
No kernel may reach another device: no remote copies, remote signals or barrier semaphores. Data moves between devices by JAX's collectives and lax.ppermute only.
A program may use at most 448 MiB of HBM per device.

v0:
```python
import jax
import jax.numpy as jnp
from jax import lax
from jax.sharding import PartitionSpec as P

H = 17
HD = 64


EPSILON = 1e-05
NEGATIVE = -1e30


def prefix(shard, axis, combine, identity):
    size, mine = (lax.axis_size(axis), lax.axis_index(axis))
    everything = lax.all_gather(shard, axis)
    start = jnp.broadcast_to(jnp.asarray(identity, shard.dtype), shard.shape)

    def step(k, before):
        reached = k < mine
        new = combine(before, everything[k])
        return jnp.where(reached, new, before)

    return lax.fori_loop(0, size, step, start)


def normed(values, gain, shift):
    centre = values - jnp.mean(values, axis=-1, keepdims=True)
    spread = jnp.mean(centre * centre, axis=-1, keepdims=True)
    return centre * lax.rsqrt(spread + EPSILON) * gain + shift


def gelu_tanh(values):
    return jax.nn.gelu(values, approximate=True)


def add_counts(earlier, later):
    return earlier + later


def allowed_pairs(query_segment, query_place, key_segment, key_place):
    return (
        (query_segment[:, None] == key_segment[None, :])
        & (key_place[None, :] <= query_place[:, None])
    )[:, None, :]


def score_pairs(query_rows, key_rows, scaling):
    return (
        jnp.einsum("qhd,khd->qhk", query_rows, key_rows, preferred_element_type=jnp.float32)
        * scaling
    )


def contract_rows(left, right):
    return lax.dot_general(
        left, right, (((0,), (0,)), ((), ())), preferred_element_type=jnp.float32
    )


def contract_cols(left, right):
    return lax.dot_general(
        left, right, (((1,), (1,)), ((), ())), preferred_element_type=jnp.float32
    )


def local(
    block_in,
    doc_flags,
    ln1_gain,
    ln1_bias,
    w_qkv,
    qv_bias,
    w_out,
    out_bias,
    ln2_gain,
    ln2_bias,
    w_up,
    up_bias,
    w_down,
    down_bias,
    cotangent,
):
    tok_rows = block_in.shape[1]
    model_width = block_in.shape[2]
    scaling = HD ** (-0.5)
    ctx_count = lax.axis_size("ctx")
    running_count = jnp.cumsum(doc_flags[0])
    offset_count = prefix(running_count[-1], "ctx", add_counts, jnp.int32(0))
    local_segment = running_count + offset_count - 1
    local_place = lax.axis_index("ctx") * tok_rows + jnp.arange(tok_rows, dtype=jnp.int32)
    (
        gain_one,
        shift_one,
        qkv_full,
        qv_full,
        out_full,
        out_shift,
        gain_two,
        shift_two,
        up_full,
        up_shift,
        down_full,
        down_shift,
    ) = (
        lax.all_gather(ln1_gain, "wsh", axis=0, tiled=True),
        lax.all_gather(ln1_bias, "wsh", axis=0, tiled=True),
        lax.all_gather(w_qkv, "wsh", axis=0, tiled=True),
        lax.all_gather(qv_bias, "wsh", axis=0, tiled=True),
        lax.all_gather(w_out, "wsh", axis=0, tiled=True),
        lax.all_gather(out_bias, "wsh", axis=0, tiled=True),
        lax.all_gather(ln2_gain, "wsh", axis=0, tiled=True),
        lax.all_gather(ln2_bias, "wsh", axis=0, tiled=True),
        lax.all_gather(w_up, "wsh", axis=1, tiled=True),
        lax.all_gather(up_bias, "wsh", axis=0, tiled=True),
        lax.all_gather(w_down, "wsh", axis=0, tiled=True),
        lax.all_gather(down_bias, "wsh", axis=0, tiled=True),
    )
    gain_one, shift_one, gain_two, shift_two = [
        vector.astype(jnp.float32) for vector in (gain_one, shift_one, gain_two, shift_two)
    ]
    out_shift, up_shift, down_shift = [
        vector.astype(jnp.float32) for vector in (out_shift, up_shift, down_shift)
    ]
    input_rows = block_in[0].astype(jnp.float32)
    normed_one = normed(input_rows, gain_one, shift_one).astype(jnp.bfloat16)
    qkv_shift = jnp.concatenate(
        [qv_full[:model_width], jnp.zeros((model_width,), qv_full.dtype), qv_full[model_width:]]
    ).astype(jnp.float32)
    projected = (
        jnp.dot(normed_one, qkv_full, preferred_element_type=jnp.float32) + qkv_shift
    ).astype(jnp.bfloat16)
    queries = projected[:, :model_width].reshape(tok_rows, H, HD)
    key_rows = projected[:, model_width : 2 * model_width].reshape(tok_rows, H, HD)
    value_rows = projected[:, 2 * model_width :].reshape(tok_rows, H, HD)
    key_piece = lax.all_gather(key_rows, "ctx", axis=0, tiled=True)
    value_piece = lax.all_gather(value_rows, "ctx", axis=0, tiled=True)
    segment_piece = lax.all_gather(local_segment, "ctx", axis=0, tiled=True)
    piece_place = jnp.arange(key_piece.shape[0], dtype=jnp.int32)
    row_best = jnp.full((tok_rows, H), NEGATIVE, jnp.float32)
    score_block = score_pairs(queries, key_piece, scaling)
    allowed = allowed_pairs(local_segment, local_place, segment_piece, piece_place)
    new_best = jnp.maximum(row_best, jnp.max(jnp.where(allowed, score_block, NEGATIVE), axis=-1))
    weight_block = jnp.where(allowed, jnp.exp(score_block - new_best[..., None]), 0.0)
    row_total = jnp.sum(weight_block, axis=-1)
    weighted = jnp.einsum(
        "qhk,khd->qhd",
        weight_block.astype(jnp.bfloat16),
        value_piece,
        preferred_element_type=jnp.float32,
    )
    row_best, row_total, weighted = (new_best, row_total, weighted)
    log_total = row_best + jnp.log(row_total)
    attended = weighted / row_total[..., None]
    attended_low = attended.reshape(tok_rows, model_width).astype(jnp.bfloat16)
    attn_branch = jnp.dot(attended_low, out_full, preferred_element_type=jnp.float32) + out_shift
    residual = input_rows + attn_branch
    normed_two = normed(residual, gain_two, shift_two).astype(jnp.bfloat16)
    hidden_pre = jnp.dot(normed_two, up_full, preferred_element_type=jnp.float32) + up_shift
    hidden_act = gelu_tanh(hidden_pre).astype(jnp.bfloat16)
    mlp_sum = jnp.dot(hidden_act, down_full, preferred_element_type=jnp.float32)
    mlp_branch = mlp_sum + down_shift
    block_full = residual + mlp_branch
    square_sums = lax.psum(
        jnp.stack(
            [
                jnp.sum(attn_branch * attn_branch),
                jnp.sum(mlp_branch * mlp_branch),
                jnp.sum(block_full * block_full),
            ]
        ),
        "ctx",
    )
    rms_values = jnp.sqrt(square_sums / (tok_rows * ctx_count * model_width)).reshape(1, 3)
    out_grad = cotangent[0].astype(jnp.float32)
    mlp_grad = out_grad.astype(jnp.bfloat16)
    grad_down_shift = jnp.sum(mlp_grad.astype(jnp.float32), axis=0)
    grad_down = contract_rows(hidden_act, mlp_grad)
    act_grad = contract_cols(mlp_grad, down_full)
    unused_act, gelu_pull = jax.vjp(gelu_tanh, hidden_pre)
    pre_grad = gelu_pull(act_grad)[0].astype(jnp.bfloat16)
    grad_up_shift = jnp.sum(pre_grad.astype(jnp.float32), axis=0)
    grad_up = contract_rows(normed_two, pre_grad)
    normed_two_grad = contract_cols(pre_grad, up_full)
    unused_two, norm_two_pull = jax.vjp(normed, residual, gain_two, shift_two)
    residual_ln, grad_gain_two, grad_shift_two = norm_two_pull(normed_two_grad)
    residual_grad = out_grad + residual_ln
    attn_grad = residual_grad.astype(jnp.bfloat16)
    grad_out_shift = jnp.sum(attn_grad.astype(jnp.float32), axis=0)
    grad_out = contract_rows(attended_low, attn_grad)
    attended_grad = contract_cols(attn_grad, out_full).astype(jnp.bfloat16).reshape(tok_rows, H, HD)
    row_delta = jnp.sum(attended_grad.astype(jnp.float32) * attended, axis=-1)
    key_piece = lax.all_gather(key_rows, "ctx", axis=0, tiled=True)
    value_piece = lax.all_gather(value_rows, "ctx", axis=0, tiled=True)
    segment_piece = lax.all_gather(local_segment, "ctx", axis=0, tiled=True)
    piece_place = jnp.arange(key_piece.shape[0], dtype=jnp.int32)
    score_block = score_pairs(queries, key_piece, scaling)
    allowed = allowed_pairs(local_segment, local_place, segment_piece, piece_place)
    probability = jnp.where(allowed, jnp.exp(score_block - log_total[..., None]), 0.0)
    prob_grad = jnp.einsum(
        "qhd,khd->qhk", attended_grad, value_piece, preferred_element_type=jnp.float32
    )
    score_grad = (probability * (prob_grad - row_delta[..., None])).astype(jnp.bfloat16)
    query_grad = scaling * jnp.einsum(
        "qhk,khd->qhd", score_grad, key_piece, preferred_element_type=jnp.float32
    )
    query_piece = lax.all_gather(
        queries.astype(jnp.float32).astype(jnp.bfloat16), "ctx", axis=0, tiled=True
    ).astype(jnp.float32)
    grad_piece = lax.all_gather(
        attended_grad.astype(jnp.float32).astype(jnp.bfloat16), "ctx", axis=0, tiled=True
    )
    total_piece = lax.all_gather(log_total.astype(jnp.bfloat16), "ctx", axis=0, tiled=True).astype(
        jnp.float32
    )
    delta_piece = lax.all_gather(row_delta.astype(jnp.bfloat16), "ctx", axis=0, tiled=True).astype(
        jnp.float32
    )
    segment_piece = lax.all_gather(local_segment, "ctx", axis=0, tiled=True)
    query_low = query_piece.astype(jnp.bfloat16)
    piece_place = jnp.arange(query_piece.shape[0], dtype=jnp.int32)
    score_block = score_pairs(query_low, key_rows, scaling)
    allowed = allowed_pairs(segment_piece, piece_place, local_segment, local_place)
    probability = jnp.where(allowed, jnp.exp(score_block - total_piece[..., None]), 0.0)
    value_grad = jnp.einsum(
        "qhk,qhd->khd",
        probability.astype(jnp.bfloat16),
        grad_piece,
        preferred_element_type=jnp.float32,
    )
    prob_grad = jnp.einsum(
        "qhd,khd->qhk", grad_piece, value_rows, preferred_element_type=jnp.float32
    )
    score_grad = (probability * (prob_grad - delta_piece[..., None])).astype(jnp.bfloat16)
    key_grad = scaling * jnp.einsum(
        "qhk,qhd->khd", score_grad, query_low, preferred_element_type=jnp.float32
    )
    key_grad, value_grad = (key_grad, value_grad)
    qkv_grad = jnp.concatenate(
        [
            query_grad.reshape(tok_rows, model_width),
            key_grad.reshape(tok_rows, model_width),
            value_grad.reshape(tok_rows, model_width),
        ],
        axis=1,
    ).astype(jnp.bfloat16)
    qkv_grad_wide = qkv_grad.astype(jnp.float32)
    grad_qv_shift = jnp.concatenate(
        [
            jnp.sum(qkv_grad_wide[:, :model_width], axis=0),
            jnp.sum(qkv_grad_wide[:, 2 * model_width :], axis=0),
        ]
    )
    grad_qkv = contract_rows(normed_one, qkv_grad)
    normed_one_grad = contract_cols(qkv_grad, qkv_full)
    unused_one, norm_one_pull = jax.vjp(normed, input_rows, gain_one, shift_one)
    input_ln, grad_gain_one, grad_shift_one = norm_one_pull(normed_one_grad)
    input_grad = (residual_grad + input_ln).astype(jnp.bfloat16)
    (
        sum_gain_one,
        sum_shift_one,
        sum_qkv,
        sum_qv_shift,
        sum_out,
        sum_out_shift,
        sum_gain_two,
        sum_shift_two,
        sum_up,
        sum_up_shift,
        sum_down,
        sum_down_shift,
    ) = (
        lax.psum_scatter(
            grad_gain_one.astype(jnp.bfloat16), "wsh", scatter_dimension=0, tiled=True
        ).astype(jnp.float32),
        lax.psum_scatter(
            grad_shift_one.astype(jnp.bfloat16), "wsh", scatter_dimension=0, tiled=True
        ).astype(jnp.float32),
        lax.psum_scatter(
            grad_qkv.astype(jnp.bfloat16), "wsh", scatter_dimension=0, tiled=True
        ).astype(jnp.float32),
        lax.psum_scatter(
            grad_qv_shift.astype(jnp.bfloat16), "wsh", scatter_dimension=0, tiled=True
        ).astype(jnp.float32),
        lax.psum_scatter(
            grad_out.astype(jnp.bfloat16), "wsh", scatter_dimension=0, tiled=True
        ).astype(jnp.float32),
        lax.psum_scatter(
            grad_out_shift.astype(jnp.bfloat16), "wsh", scatter_dimension=0, tiled=True
        ).astype(jnp.float32),
        lax.psum_scatter(
            grad_gain_two.astype(jnp.bfloat16), "wsh", scatter_dimension=0, tiled=True
        ).astype(jnp.float32),
        lax.psum_scatter(
            grad_shift_two.astype(jnp.bfloat16), "wsh", scatter_dimension=0, tiled=True
        ).astype(jnp.float32),
        lax.psum_scatter(
            grad_up.astype(jnp.bfloat16), "wsh", scatter_dimension=1, tiled=True
        ).astype(jnp.float32),
        lax.psum_scatter(
            grad_up_shift.astype(jnp.bfloat16), "wsh", scatter_dimension=0, tiled=True
        ).astype(jnp.float32),
        lax.psum_scatter(
            grad_down.astype(jnp.bfloat16), "wsh", scatter_dimension=0, tiled=True
        ).astype(jnp.float32),
        lax.psum_scatter(
            grad_down_shift.astype(jnp.bfloat16), "wsh", scatter_dimension=0, tiled=True
        ).astype(jnp.float32),
    )
    totals = lax.psum(
        (
            sum_gain_one,
            sum_shift_one,
            sum_qkv,
            sum_qv_shift,
            sum_out,
            sum_out_shift,
            sum_gain_two,
            sum_shift_two,
            sum_up,
            sum_up_shift,
            sum_down,
            sum_down_shift,
        ),
        "ctx",
    )
    return (
        block_full.astype(jnp.bfloat16)[None],
        input_grad[None],
        totals[0],
        totals[1],
        totals[2],
        totals[3],
        totals[4],
        totals[5],
        totals[6],
        totals[7],
        totals[8],
        totals[9],
        totals[10],
        totals[11],
        rms_values,
    )


def solution(mesh):
    return jax.shard_map(
        local,
        mesh=mesh,
        in_specs=(
            P("wsh", "ctx", None),
            P("wsh", "ctx"),
            P("wsh"),
            P("wsh"),
            P("wsh", None),
            P("wsh"),
            P("wsh", None),
            P("wsh"),
            P("wsh"),
            P("wsh"),
            P(None, "wsh"),
            P("wsh"),
            P("wsh", None),
            P("wsh"),
            P("wsh", "ctx", None),
        ),
        out_specs=(
            P("wsh", "ctx", None),
            P("wsh", "ctx", None),
            P("wsh"),
            P("wsh"),
            P("wsh", None),
            P("wsh"),
            P("wsh", None),
            P("wsh"),
            P("wsh"),
            P("wsh"),
            P(None, "wsh"),
            P("wsh"),
            P("wsh", None),
            P("wsh"),
            P("wsh", None),
        ),
        check_vma=False,
    )
```

profile of v0, /device:TPU:0, one launch (start us, length us, event | category | flops | bytes accessed | tf_op | source)
XLA Modules:
  0.0 1312.9 jit_solution(13402227410424591593)
XLA Ops:
  8.0 1.3 fusion.106
  17.4 0.9 dynamic-update-slice.7
  18.2 14.6 %all-reduce.19 = (bf16[2176]{0:T(1024)(128)(2,1)S(1)}, bf16[1088]{0:T(1024)(128)(2,1)S(1)}, bf16[1088]{0:T(1024)(128)(2,1)S(1)}, bf16[1088]{0:T(1024)(128)(2,1)S...) all-reduce(bf16[2176]{0:T(1024)(128)(2,1)S(1)} %dynamic-update-slic, ...), channel_id=1, replica_groups=mesh['ctx'=8,'wsh'=4] {'wsh'}, use_global_device_ids=true, to_apply=%add.2 | all-reduce | flops 13056 | bytes 52224
  33.4 31.6 %all-gather.11.cloned.1.call-done = bf16[1088,3264]{1,0:T(8,128)(2,1)} async-done(((bf16[272,3264]{1,0:T(8,128)(2,1)}), bf16[1088,3264]{1,0:T(8,128)(2,1)}) %all-gather.11.cloned.1.call-update) | async-done | bytes 7102480 | tf_op jit(solution)/shard_map/all_gather | solution.py:108
  64.9 6.4 fusion.14
  71.4 0.9 fusion.104
  73.7 3.2 copy.42
  79.0 1.3 bitcast_dynamic-update-slice_fusion
  80.3 11.5 all-reduce.3
  91.8 10.1 while.13
  102.0 32.7 %all-gather.1 = s32[1024,1]{1,0:T(8,128)S(1)} all-gather(s32[128,1]{1,0:T(8,128)S(1)} %get-tuple-element.154), channel_id=3, replica_groups=mesh['ctx'=8,'wsh'=4] {'ctx'}, dimensions={0}, use_global_device_ids=true | all-gather | bytes 4608 | tf_op jit(solution)/shard_map/all_gather | solution.py:138
  136.4 3.7 fusion.6
  140.1 3.4 copy-done.1
  143.5 1.8 fusion.11
  145.4 41.0 %all-gather.13.cloned.1.call-done = bf16[1024,17,64]{0,2,1:T(8,128)(2,1)} async-done(((bf16[128,17,64]{0,2,1:T(8,128)(2,1)}), bf16[1024,17,64]{0,2,1:T(8,128)(2,1)}) %all-gather.13.cloned.1.call-update) | async-done | bytes 2228240 | tf_op jit(solution)/shard_map/all_gather | solution.py:137
  186.3 6.8 fusion.107
  193.2 17.7 %all-gather.17.cloned.1.call-done = bf16[1088,1088]{1,0:T(8,128)(2,1)} async-done(((bf16[272,1088]{1,0:T(8,128)(2,1)}), bf16[1088,1088]{1,0:T(8,128)(2,1)}) %all-gather.17.cloned.1.call-update) | async-done | bytes 2367504 | tf_op jit(solution)/shard_map/all_gather | solution.py:110
  210.9 3.5 fusion.101
  215.9 64.6 %all-gather.19.cloned.1.call-done = bf16[1088,4352]{0,1:T(8,128)(2,1)} async-done(((bf16[1088,1088]{0,1:T(8,128)(2,1)}), bf16[1088,4352]{0,1:T(8,128)(2,1)}) %all-gather.19.cloned.1.call-update) | async-done | bytes 9469968 | tf_op jit(solution)/shard_map/all_gather | solution.py:114
  280.5 7.2 convolution_add_fusion
  287.7 61.8 %all-gather.21.cloned.1.call-done = bf16[4352,1088]{1,0:T(8,128)(2,1)} async-done(((bf16[1088,1088]{1,0:T(8,128)(2,1)}), bf16[4352,1088]{1,0:T(8,128)(2,1)}) %all-gather.21.cloned.1.call-update) | async-done | bytes 9469968 | tf_op jit(solution)/shard_map/all_gather | solution.py:116
  349.5 7.8 fusion.108
  357.3 4.0 fusion.109
  361.4 9.2 multiply_reduce_fusion.1
  371.2 1.5 copy-done.9
  372.7 1.5 convolution_convert_fusion.4
  374.3 3.3 convolution_convert_fusion.3
  379.2 26.6 %all_gather.81 = bf16[1024,17]{0,1:T(8,128)(2,1)S(1)} all-gather(bf16[128,17]{0,1:T(8,128)(2,1)S(1)} %get-tuple-element.147), channel_id=1, replica_groups=mesh['ctx'=8,'wsh'=4] {'ctx'}, dimensions={0}, use_global_device_ids=true | all-gather | bytes 39168 | tf_op jit(solution)/shard_map/all_gather | solution.py:213
  406.4 1.2 multiply_reduce_fusion.4
  407.6 26.3 %all_gather.83 = bf16[1024,17]{0,1:T(8,128)(2,1)S(1)} all-gather(bf16[128,17]{0,1:T(8,128)(2,1)S(1)} %convert_element_type.201), channel_id=1, replica_groups=mesh['ctx'=8,'wsh'=4] {'ctx'}, dimensions={0}, use_global_device_ids=true | all-gather | bytes 39168 | tf_op jit(solution)/shard_map/all_gather | solution.py:216
  434.6 6.6 fusion.110
  441.2 9.5 fusion.47
  450.7 7.4 all-gather.25.cloned.1.call-done
  458.0 6.7 fusion.53
  464.8 10.5 fusion.50
  475.3 6.6 convolution_convert_fusion.2
  482.5 6.7 convolution_convert_fusion.1
  489.3 14.0 %copy.50 = bf16[1088,4352]{0,1:T(8,128)(2,1)} copy(bf16[1088,4352]{1,0:T(8,128)(2,1)} %convolution_convert_fusion.1) | data formatting | bytes 18939904
  503.4 6.2 convolution_convert_fusion
  511.8 2.0 pad_maximum_fusion.2
  514.5 5.3 fusion.96
  520.2 13.2 %all-reduce.18 = (bf16[1088]{0:T(1024)(128)(2,1)S(1)}, bf16[1088]{0:T(1024)(128)(2,1)S(1)}, bf16[2176]{0:T(1024)(128)(2,1)S(1)}, bf16[1088]{0:T(1024)(128)(2,1)S...) all-reduce(bf16[1088]{0:T(1024)(128)(2,1)S(1)} %get-tuple-element.9, ...), channel_id=4, replica_groups=mesh['ctx'=8,'wsh'=4] {'wsh'}, use_global_device_ids=true, to_apply=%region_15.16.clone | all-reduce | flops 13056 | bytes 52224
  533.8 1.0 fusion.75
  534.8 26.8 %reduce-scatter.7.cloned.1.call-done = bf16[272,3264]{1,0:T(8,128)(2,1)} async-done(((bf16[1088,3264]{1,0:T(8,128)(2,1)}), bf16[272,3264]{1,0:T(8,128)(2,1)}) %reduce-scatter.7.cloned.1.call-update) | async-done | bytes 1775632 | tf_op jit(solution)/shard_map/reduce_scatter | solution.py:279
  561.6 84.9 %reduce-scatter.13.cloned.1.call-done = bf16[1088,1088]{1,0:T(8,128)(2,1)} async-done(((bf16[4352,1088]{1,0:T(8,128)(2,1)}), bf16[1088,1088]{1,0:T(8,128)(2,1)}) %reduce-scatter.13.cloned.1.call-update) | async-done | bytes 2367504
  646.5 4.1 copy.51
  650.7 80.6 %reduce-scatter.11.cloned.1.call-done = bf16[1088,1088]{1,0:T(8,128)(2,1)} async-done(((bf16[4352,1088]{1,0:T(8,128)(2,1)}), bf16[1088,1088]{1,0:T(8,128)(2,1)}) %reduce-scatter.11.cloned.1.call-update) | async-done | bytes 2367504 | tf_op jit(solution)/shard_map/reduce_scatter | solution.py:303
  731.3 573.8 %all-reduce.21 = (f32[272]{0:T(512)}, f32[272]{0:T(512)}, f32[272,3264]{1,0:T(8,128)}, f32[544]{0:T(1024)}, f32[272,1088]{1,0:T(8,128)}, /*index=5*/f32[272]{0:T...) all-reduce(f32[272]{0:T(512)S(1)} %get-tuple-element.176, ...), channel_id=1, replica_groups=mesh['ctx'=8,'wsh'=4] {'ctx'}, use_global_device_ids=true, to_apply=%region_16.17 | all-reduce | flops 3554499 | bytes 21333528 | tf_op jit(solution)/shard_map/psum | solution.py:310
  (182 shorter events, 25.0 us)
Async XLA Ops:
  7.2 25.8 %copy-start.2 = (bf16[1,128,1088]{1,2,0:T(8,128)(2,1)S(1)}, bf16[1,128,1088]{1,2,0:T(8,128)(2,1)}, u32[]{:S(2)}) copy-start(bf16[1,128,1088]{1,2,0:T(8,128)(2,1)} %param.17) | copy-start | bytes 835588
  7.2 57.8 %all-gather.11.cloned.1.call-start = ((), (), s32[]{:S(2)}) async-start(), calls=%async_computation.4 | async-start | bytes 9052160 | tf_op jit(solution)/shard_map/all_gather | solution.py:108
  7.9 128.4 %all-gather.15.cloned.1.call-start = ((), (), s32[]{:S(2)}) async-start(), calls=%async_computation.6 | async-start | bytes 2506752 | tf_op jit(solution)/shard_map/all_gather | solution.py:136
  33.2 38.2 %copy-start.17 = (f32[128]{0:T(128)}, f32[128]{0:T(128)S(1)}, u32[]{:S(2)}) copy-start(f32[128]{0:T(128)S(1)} %broadcast_multiply_fusion.1) | copy-start | bytes 1540
  33.3 38.0 %copy-start.37 = (f32[128]{0:T(128)}, f32[128]{0:T(128)S(1)}, u32[]{:S(2)}) copy-start(f32[128]{0:T(128)S(1)} %fusion.70) | copy-start | bytes 1540
  33.4 38.0 %copy-start.21 = (f32[128]{0:T(128)}, f32[128]{0:T(128)S(1)}, u32[]{:S(2)}) copy-start(f32[128]{0:T(128)S(1)} %fusion.82) | copy-start | bytes 1540
  71.4 2.3 copy-start.8
  72.3 114.0 %all-gather.13.cloned.1.call-start = ((), (), s32[]{:S(2)}) async-start(), calls=%async_computation.5 | async-start | bytes 2506752 | tf_op jit(solution)/shard_map/all_gather | solution.py:137
  73.1 137.8 %all-gather.17.cloned.1.call-start = ((), (), s32[]{:S(2)}) async-start(), calls=%async_computation.7 | async-start | bytes 3133440 | tf_op jit(solution)/shard_map/all_gather | solution.py:110
  73.7 206.8 %all-gather.19.cloned.1.call-start = ((), (), s32[]{:S(2)}) async-start(), calls=%async_computation.8 | async-start | bytes 12533760 | tf_op jit(solution)/shard_map/all_gather | solution.py:114
  77.0 59.4 %copy-start.7 = (bf16[128,1088]{0,1:T(8,128)(2,1)S(1)}, bf16[128,1088]{0,1:T(8,128)(2,1)}, u32[]{:S(2)}) copy-start(bf16[128,1088]{0,1:T(8,128)(2,1)} %get-tuple-element.156) | copy-start | bytes 835588
  77.0 272.6 %all-gather.21.cloned.1.call-start = ((), (), s32[]{:S(2)}) async-start(), calls=%async_computation.9 | async-start | bytes 12533760 | tf_op jit(solution)/shard_map/all_gather | solution.py:116
  77.5 357.1 %all-gather.23.cloned.1.call-start = ((), (), s32[]{:S(2)}) async-start(), calls=%async_computation.10 | async-start | bytes 2506752 | tf_op jit(solution)/shard_map/all_gather | solution.py:207
  102.0 34.3 %copy-start.28 = (s32[128]{0:T(128)}, s32[128]{0:T(128)S(1)}, u32[]{:S(2)}) copy-start(s32[128]{0:T(128)S(1)} %get-tuple-element.153) | copy-start | bytes 1540
  135.8 322.2 %all-gather.25.cloned.1.call-start = ((), (), s32[]{:S(2)}) async-start(), calls=%async_computation.11 | async-start | bytes 2506752 | tf_op jit(solution)/shard_map/all_gather | solution.py:210
  140.1 3.5 copy-start.1
  193.2 21.3 %copy-start.14 = (bf16[128,17,64]{0,2,1:T(8,128)(2,1)}, bf16[128,17,64]{0,2,1:T(8,128)(2,1)S(1)}, u32[]{:S(2)}) copy-start(bf16[128,17,64]{0,2,1:T(8,128)(2,1)S(1)} %get-tuple-element.166) | copy-start | bytes 835588
  215.9 133.7 %copy-start.6 = (bf16[1,128,1088]{1,2,0:T(8,128)(2,1)S(1)}, bf16[1,128,1088]{1,2,0:T(8,128)(2,1)}, u32[]{:S(2)}) copy-start(bf16[1,128,1088]{1,2,0:T(8,128)(2,1)} %param.31) | copy-start | bytes 835588
  349.5 7.8 copy-start
  357.3 4.0 copy-start.5
  357.3 4.0 copy-start.20
  357.3 4.0 copy-start.25
  357.3 4.1 copy-start.27
  361.4 9.3 copy-start.40
  370.6 2.0 copy-start.9
  370.9 3.3 copy-start.3
  370.9 3.3 copy-start.32
  371.2 3.0 copy-start.13
  374.2 3.5 copy-start.29
  374.3 3.5 copy-start.35
  374.3 160.5 %reduce-scatter.9.cloned.1.call-start = ((), (), s32[]{:S(2)}) async-start(), calls=%async_computation.13 | async-start | bytes 3133440 | tf_op jit(solution)/shard_map/reduce_scatter | solution.py:285
  377.7 183.9 %reduce-scatter.7.cloned.1.call-start = ((), (), s32[]{:S(2)}) async-start(), calls=%async_computation.12 | async-start | bytes 9052160 | tf_op jit(solution)/shard_map/reduce_scatter | solution.py:279
  434.6 6.6 copy-start.23
  450.7 14.1 %copy-start.16 = (pred[1024,128]{0,1:T(8,128)(4,1)S(1)}, pred[1024,128]{0,1:T(8,128)(4,1)}, u32[]{:S(2)}) copy-start(pred[1024,128]{0,1:T(8,128)(4,1)} %fusion.73) | copy-start | bytes 393220
  464.8 10.5 copy-start.18
  464.8 10.5 copy-start.22
  481.9 164.6 %reduce-scatter.13.cloned.1.call-start = ((), (), s32[]{:S(2)}) async-start(), calls=%async_computation.15 | async-start | bytes 12533760
  503.3 228.0 %reduce-scatter.11.cloned.1.call-start = ((), (), s32[]{:S(2)}) async-start(), calls=%async_computation.14 | async-start | bytes 12533760 | tf_op jit(solution)/shard_map/reduce_scatter | solution.py:303
  509.6 4.3 copy-start.10
  509.6 4.3 copy-start.11
  509.6 4.3 copy-start.12
  514.5 5.3 copy-start.38
  514.5 5.7 copy-start.24
  514.5 5.7 copy-start.30
  514.5 5.8 copy-start.31
  514.5 19.4 %copy-start.4 = (f32[128,1088]{0,1:T(8,128)S(1)}, f32[128,1088]{0,1:T(8,128)}, u32[]{:S(2)}) copy-start(f32[128,1088]{0,1:T(8,128)} %copy-done.3) | copy-start | bytes 1671172
  514.5 19.3 %copy-start.33 = (f32[128]{0:T(128)S(1)}, f32[128]{0:T(128)}, u32[]{:S(2)}) copy-start(f32[128]{0:T(128)} %copy-done.32) | copy-start | bytes 1540
  646.5 84.8 %copy-start.15 = (bf16[272,1088]{1,0:T(8,128)(2,1)S(1)}, bf16[272,1088]{1,0:T(8,128)(2,1)}, u32[]{:S(2)}) copy-start(bf16[272,1088]{1,0:T(8,128)(2,1)} %reduce-scatter.9.cloned.1.call-done) | copy-start | bytes 1775620
  (6 other events, 3.9 us)
Sparse Core Ops, SparseCore 0:
  9.6 55.3 all-gather.10
  72.5 60.5 all-gather.14
  135.1 51.2 all-gather.12
  187.7 23.0 all-gather.16
  212.9 67.5 all-gather.18
  281.9 67.5 all-gather.20
  352.1 53.1 all-gather.22
  407.4 50.6 all-gather.24
  461.2 32.1 reduce-scatter.8
  496.0 65.5 reduce-scatter.6
  564.2 82.2 reduce-scatter.12
  649.0 82.2 reduce-scatter.10
where the time goes:
time: 1320 us; the launch traced here: 1310 us
  blocking collectives  699 us (53%)
  waiting for transfers between devices  419 us (32%)
  matrix products  112 us (8%)
  local copies, waits for them, and re-layouts  44.5 us (3%)
  between operations  19.1 us (1%)
  other arithmetic  13.7 us (1%)
    psum x1, blocking collectives, local(): lax.psum((sum_gain_one, sum_shift_one, sum_qkv, sum_qv_shift, sum_out, su...  574 us
    unnamed x13, waiting for transfers between devices  87.5 us
    reduce_scatter x1, waiting for transfers between devices, local(): lax.psum_scatter(grad_down.astype(jnp.bfloat16), 'wsh', scatter_dimension...  80.6 us
    all_gather x1, waiting for transfers between devices, local(): lax.all_gather(w_up, 'wsh', axis=1, tiled=True)  64.6 us
    all_gather x1, waiting for transfers between devices, local(): lax.all_gather(w_down, 'wsh', axis=0, tiled=True)  61.8 us
    all_gather x1, waiting for transfers between devices, local(): value_piece = lax.all_gather(value_rows, 'ctx', axis=0, tiled=True)  41 us
    unnamed x108, local copies, waits for them, and re-layouts  38.1 us
    all_gather x1, blocking collectives, local(): segment_piece = lax.all_gather(local_segment, 'ctx', axis=0, tiled=True)  32.7 us
  transfers between devices with their start and end apart: 12, of which 9 were waited for; matrix products, arithmetic and copies ran while one was open for 12% of the time, Pallas kernels for 0%

commit v1 on v0

--- a/solution.py
+++ b/solution.py
@@ -1,14 +1,773 @@
+import functools
+import math
+
 import jax
 import jax.numpy as jnp
 from jax import lax
+from jax.experimental import pallas as pl
+from jax.experimental.pallas import tpu as pltpu
 from jax.sharding import PartitionSpec as P
 
 H = 17
 HD = 64
-
-
+LANES = 128
 EPSILON = 1e-05
 NEGATIVE = -1e30
+LOG2E = math.log2(math.e)
+SCORE_SCALE = HD ** (-0.5) * LOG2E
+VMEM_MOST = 56 * 2**20
+
+F32 = jnp.float32
+BF16 = jnp.bfloat16
+
+
+def dot_nn(left, right):
+    return lax.dot_general(left, right, (((1,), (0,)), ((), ())), preferred_element_type=F32)
+
+
+def dot_nt(left, right):
+    return lax.dot_general(left, right, (((1,), (1,)), ((), ())), preferred_element_type=F32)
+
+
+def dot_tn(left, right):
+    return lax.dot_general(left, right, (((0,), (0,)), ((), ())), preferred_element_type=F32)
+
+
+def swap(value, axis, distance):
+    size = lax.axis_size(axis)
+    return lax.ppermute(value, axis, [(i, i ^ distance) for i in range(size)])
+
+
+def centred(values):
+    centre = values - jnp.mean(values, axis=-1, keepdims=True)
+    spread = jnp.mean(centre * centre, axis=-1, keepdims=True)
+    return centre, lax.rsqrt(spread + EPSILON)
+
+
+def norm_back(unit, inverse, scaled_grad):
+    mean_grad = jnp.mean(scaled_grad, axis=-1, keepdims=True)
+    mean_both = jnp.mean(scaled_grad * unit, axis=-1, keepdims=True)
+    return inverse * (scaled_grad - mean_grad - unit * mean_both)
+
+
+QB = 256
+
+
+def head_lanes(head):
+    lane = lax.broadcasted_iota(jnp.int32, (1, LANES), 1)
+    return (lane >= HD * head) & (lane < HD * (head + 1))
+
+
+def masked_scores(keys, queries, start_row, key_at, query_at):
+    scores = dot_nt(keys, queries) * SCORE_SCALE
+    shape = scores.shape
+    key_place = lax.broadcasted_iota(jnp.int32, shape, 0) + key_at
+    allowed = key_place >= start_row
+    if key_at + shape[0] > query_at:
+        query_place = lax.broadcasted_iota(jnp.int32, shape, 1) + query_at
+        allowed = allowed & (key_place <= query_place)
+    return jnp.where(allowed, scores, NEGATIVE)
+
+
+def fold_rows(values, combine):
+    return combine(values.reshape(values.shape[0] // 8, 8, values.shape[1]), axis=0)
+
+
+def attend_forward_kernel(
+    n_ctx, n_wsh, place_ref, start_ref, gain_ref, shift_ref, bias_ref, *refs
+):
+    blocks, refs = refs[:n_ctx], refs[n_ctx:]
+    weights, refs = refs[:n_wsh], refs[n_wsh:]
+    normed_ref, qkv_ref, attended_ref, total_ref, own_ref, *refs = refs
+    sends, (weight_ref, score_ref, prob_ref, value_ref) = refs[:n_ctx], refs[n_ctx:]
+    ctx, wsh = place_ref[0], place_ref[1]
+    tok_rows = blocks[0].shape[0]
+    length = n_ctx * tok_rows
+    weight_rows = weights[0].shape[0]
+    for k in range(n_wsh):
+        at = pl.multiple_of((wsh ^ k) * weight_rows, 16)
+        weight_ref[pl.ds(at, weight_rows), :] = weights[k][...]
+    for j in range(n_ctx):
+        at = pl.multiple_of((ctx ^ j) * tok_rows, tok_rows)
+        centre, inverse = centred(blocks[j][...].astype(F32))
+        values = centre * inverse * gain_ref[...] + shift_ref[...]
+        normed_ref[pl.ds(at, tok_rows), :] = values.astype(BF16)
+    for at in range(0, length, QB):
+        rows = pl.ds(at, QB)
+        values = dot_nn(normed_ref[rows, :], weight_ref[...]) + bias_ref[...]
+        qkv_ref[rows, :] = values.astype(BF16)
+    for group in range(2):
+        value_ref[group] = qkv_ref[:, pl.ds((4 + group) * LANES, LANES)].T
+    for head in range(3):
+        group, half = head // 2, head % 2
+        for query_at in range(0, length, QB):
+            columns = pl.ds(query_at, QB)
+            queries = qkv_ref[columns, pl.ds(group * LANES, LANES)]
+            queries = jnp.where(head_lanes(half), queries, 0)
+            start_row = start_ref[:, columns]
+            best = None
+            for key_at in range(0, query_at + QB, QB):
+                keys = qkv_ref[pl.ds(key_at, QB), pl.ds((2 + group) * LANES, LANES)]
+                scores = masked_scores(keys, queries, start_row, key_at, query_at)
+                score_ref[pl.ds(key_at, QB), :] = scores
+                most = fold_rows(scores, jnp.max)
+                best = most if best is None else jnp.maximum(best, most)
+            best = jnp.max(best, axis=0, keepdims=True)
+            total = None
+            for key_at in range(0, query_at + QB, QB):
+                weight = jnp.exp2(score_ref[pl.ds(key_at, QB), :] - best)
+                some = fold_rows(weight, jnp.sum)
+                total = some if total is None else total + some
+                prob_ref[pl.ds(key_at, QB), :] = weight.astype(BF16)
+            total = jnp.sum(total, axis=0, keepdims=True)
+            reach = query_at + QB
+            values = value_ref[group, pl.ds(half * HD, HD), pl.ds(0, reach)]
+            weighted = dot_nn(values, prob_ref[pl.ds(0, reach), :])
+            attended_ref[pl.ds(head * HD, HD), columns] = weighted / total
+            total_ref[pl.ds(head, 1), columns] = best + jnp.log2(total)
+    for j in range(n_ctx):
+        at = pl.multiple_of((ctx ^ j) * tok_rows, tok_rows)
+        sends[j][...] = attended_ref[pl.ds(0, 2 * HD), pl.ds(at, tok_rows)].T.astype(BF16)
+    at = pl.multiple_of(ctx * tok_rows, tok_rows)
+    shared = attended_ref[pl.ds(2 * HD, HD), pl.ds(at, tok_rows)]
+    shared = jnp.concatenate([shared, jnp.zeros_like(shared)], axis=0)
+    own_ref[...] = shared.T.astype(BF16)
+
+
+def attend_forward(place, start_row, gain, shift, bias, blocks, weights):
+    n_ctx, n_wsh = len(blocks), len(weights)
+    tok_rows, width = blocks[0].shape
+    length = n_ctx * tok_rows
+    columns = weights[0].shape[1]
+    shapes = [
+        jax.ShapeDtypeStruct((length, width), BF16),
+        jax.ShapeDtypeStruct((length, columns), BF16),
+        jax.ShapeDtypeStruct((3 * HD, length), F32),
+        jax.ShapeDtypeStruct((8, length), F32),
+        jax.ShapeDtypeStruct((tok_rows, LANES), BF16),
+    ] + [jax.ShapeDtypeStruct((tok_rows, LANES), BF16)] * n_ctx
+    pairs = 3 * length * length // 2
+    out = pl.pallas_call(
+        functools.partial(attend_forward_kernel, n_ctx, n_wsh),
+        out_shape=shapes,
+        in_specs=[pl.BlockSpec(memory_space=pltpu.SMEM)]
+        + [pl.BlockSpec(memory_space=pltpu.VMEM)] * (4 + n_ctx + n_wsh),
+        out_specs=[pl.BlockSpec(memory_space=pltpu.VMEM)] * len(shapes),
+        scratch_shapes=[
+            pltpu.VMEM((width, columns), BF16),
+            pltpu.VMEM((length, QB), F32),
+            pltpu.VMEM((length, QB), BF16),
+            pltpu.VMEM((2, LANES, length), BF16),
+        ],
+        compiler_params=pltpu.CompilerParams(vmem_limit_bytes=VMEM_MOST),
+        cost_estimate=pl.CostEstimate(
+            flops=2 * length * width * columns + 4 * pairs * LANES,
+            bytes_accessed=2 * length * (2 * width + columns) + 2 * width * columns,
+            transcendentals=pairs,
+        ),
+        name="attend_forward",
+    )(place, start_row, gain, shift, bias, *blocks, *weights)
+    normed, qkv, attended, total, own, *sends = out
+    return normed, qkv, attended, total, own, sends
+
+
+def attend_backward_kernel(n_ctx, place_ref, start_ref, qkv_ref, attended_ref, total_ref, *refs):
+    grads, (all_ref, own_ref, *refs) = refs[:n_ctx], refs[n_ctx:]
+    sends, (grad_ref, key_ref, turned_ref, sum_ref, query_ref) = refs[:n_ctx], refs[n_ctx:]
+    ctx = place_ref[0]
+    tok_rows = grads[0].shape[0]
+    length = n_ctx * tok_rows
+    for j in range(n_ctx):
+        at = pl.multiple_of((ctx ^ j) * tok_rows, tok_rows)
+        grad_ref[pl.ds(at, tok_rows), :] = grads[j][...]
+    for group in range(2):
+        key_ref[group] = qkv_ref[:, pl.ds((2 + group) * LANES, LANES)].T
+        turned_ref[group] = grad_ref[:, pl.ds(group * LANES, LANES)].T
+    sum_ref[...] = jnp.zeros_like(sum_ref)
+    for head in range(3):
+        group, half = head // 2, head % 2
+        for query_at in range(0, length, QB):
+            columns = pl.ds(query_at, QB)
+            lanes = head_lanes(half)
+            queries = qkv_ref[columns, pl.ds(group * LANES, LANES)]
+            queries = jnp.where(lanes, queries, 0)
+            grad = jnp.where(lanes, grad_ref[columns, pl.ds(group * LANES, LANES)], 0)
+            start_row = start_ref[:, columns]
+            total = total_ref[pl.ds(head, 1), columns]
+            turned = turned_ref[group, pl.ds(half * HD, HD), columns].astype(F32)
+            delta = turned * attended_ref[pl.ds(head * HD, HD), columns]
+            delta = jnp.sum(delta, axis=0, keepdims=True)
+            query_grad = None
+            for key_at in range(0, query_at + QB, QB):
+                rows = pl.ds(key_at, QB)
+                keys = qkv_ref[rows, pl.ds((2 + group) * LANES, LANES)]
+                values = qkv_ref[rows, pl.ds((4 + group) * LANES, LANES)]
+                scores = masked_scores(keys, queries, start_row, key_at, query_at)
+                prob = jnp.exp2(scores - total)
+                score_grad = (prob * (dot_nt(values, grad) - delta)).astype(BF16)
+                sum_ref[1, rows, pl.ds(group * LANES, LANES)] += dot_nn(prob.astype(BF16), grad)
+                sum_ref[0, rows, pl.ds(group * LANES, LANES)] += dot_nn(score_grad, queries)
+                part = dot_nn(key_ref[group, pl.ds(half * HD, HD), rows], score_grad)
+                query_grad = part if query_grad is None else query_grad + part
+            query_ref[pl.ds(head * HD, HD), columns] = query_grad * HD ** (-0.5)
+    query_ref[pl.ds(3 * HD, HD), :] = jnp.zeros((HD, length), F32)
+    for group in range(2):
+        lanes = pl.ds(group * LANES, LANES)
+        all_ref[:, lanes] = query_ref[pl.ds(group * LANES, LANES), :].T.astype(BF16)
+        key_grad = sum_ref[0, :, lanes] * HD ** (-0.5)
+        all_ref[:, pl.ds((2 + group) * LANES, LANES)] = key_grad.astype(BF16)
+        all_ref[:, pl.ds((4 + group) * LANES, LANES)] = sum_ref[1, :, lanes].astype(BF16)
+    for part in range(3):
+        lanes = pl.ds(part * LANES, LANES)
+        for j in range(n_ctx):
+            at = pl.multiple_of((ctx ^ j) * tok_rows, tok_rows)
+            sends[j][:, lanes] = all_ref[pl.ds(at, tok_rows), pl.ds(2 * part * LANES, LANES)]
+        at = pl.multiple_of(ctx * tok_rows, tok_rows)
+        own_ref[:, lanes] = all_ref[pl.ds(at, tok_rows), pl.ds((2 * part + 1) * LANES, LANES)]
+
+
+def attend_backward(place, start_row, qkv, attended, total, grads):
+    n_ctx = len(grads)
+    tok_rows = grads[0].shape[0]
+    length = n_ctx * tok_rows
+    shapes = [
+        jax.ShapeDtypeStruct((length, 6 * LANES), BF16),
+        jax.ShapeDtypeStruct((tok_rows, 3 * LANES), BF16),
+    ] + [jax.ShapeDtypeStruct((tok_rows, 3 * LANES), BF16)] * n_ctx
+    pairs = 3 * length * length // 2
+    every, own, *sends = pl.pallas_call(
+        functools.partial(attend_backward_kernel, n_ctx),
+        out_shape=shapes,
+        in_specs=[pl.BlockSpec(memory_space=pltpu.SMEM)]
+        + [pl.BlockSpec(memory_space=pltpu.VMEM)] * (4 + n_ctx),
+        out_specs=[pl.BlockSpec(memory_space=pltpu.VMEM)] * len(shapes),
+        scratch_shapes=[
+            pltpu.VMEM((length, 2 * LANES), BF16),
+            pltpu.VMEM((2, LANES, length), BF16),
+            pltpu.VMEM((2, LANES, length), BF16),
+            pltpu.VMEM((2, length, 2 * LANES), F32),
+            pltpu.VMEM((2 * LANES, length), F32),
+        ],
+        compiler_params=pltpu.CompilerParams(vmem_limit_bytes=VMEM_MOST),
+        cost_estimate=pl.CostEstimate(
+            flops=10 * pairs * LANES,
+            bytes_accessed=2 * length * 20 * LANES,
+            transcendentals=pairs,
+        ),
+        name="attend_backward",
+    )(place, start_row, qkv, attended, total, *grads)
+    return every, own, sends
+
+
+def out_project_kernel(
+    n_ctx, n_wsh, place_ref, own_ref, in_ref, bias_ref, gain_ref, shift_ref, *refs
+):
+    parts, refs = refs[:n_ctx], refs[n_ctx:]
+    weights, refs = refs[:n_wsh], refs[n_wsh:]
+    low_ref, residual_ref, normed_ref, square_ref, weight_ref = refs
+    ctx, wsh = place_ref[0], place_ref[1]
+    weight_rows = weights[0].shape[0]
+    for k in range(n_wsh):
+        at = pl.multiple_of((wsh ^ k) * weight_rows, 16)
+        weight_ref[pl.ds(at, weight_rows), :] = weights[k][...]
+    for j in range(n_ctx):
+        at = pl.multiple_of((ctx ^ j) * LANES, LANES)
+        low_ref[:, pl.ds(at, LANES)] = parts[j][...]
+    low_ref[:, pl.ds(n_ctx * LANES, HD)] = own_ref[:, pl.ds(0, HD)]
+    branch = dot_nn(low_ref[...], weight_ref[...]) + bias_ref[...]
+    square_ref[...] = jnp.sum(branch * branch, axis=0, keepdims=True)
+    residual = in_ref[...].astype(F32) + branch
+    residual_ref[...] = residual
+    centre, inverse = centred(residual)
+    normed_ref[...] = (centre * inverse * gain_ref[...] + shift_ref[...]).astype(BF16)
+
+
+def whole_call(kernel, name, shapes, scratch, flops, place, *arrays):
+    moved = sum(a.size * a.dtype.itemsize for a in arrays)
+    moved += sum(math.prod(s.shape) * s.dtype.itemsize for s in shapes)
+    return pl.pallas_call(
+        kernel,
+        out_shape=shapes,
+        in_specs=[pl.BlockSpec(memory_space=pltpu.SMEM)]
+        + [pl.BlockSpec(memory_space=pltpu.VMEM)] * len(arrays),
+        out_specs=[pl.BlockSpec(memory_space=pltpu.VMEM)] * len(shapes),
+        scratch_shapes=scratch,
+        compiler_params=pltpu.CompilerParams(vmem_limit_bytes=VMEM_MOST),
+        cost_estimate=pl.CostEstimate(flops=flops, bytes_accessed=moved, transcendentals=0),
+        name=name,
+    )(place, *arrays)
+
+
+def out_project(place, own, rows_in, bias, gain, shift, parts, weights):
+    tok_rows, width = rows_in.shape
+    return whole_call(
+        functools.partial(out_project_kernel, len(parts), len(weights)),
+        "out_project",
+        [
+            jax.ShapeDtypeStruct((tok_rows, width), BF16),
+            jax.ShapeDtypeStruct((tok_rows, width), F32),
+            jax.ShapeDtypeStruct((tok_rows, width), BF16),
+            jax.ShapeDtypeStruct((1, width), F32),
+        ],
+        [pltpu.VMEM((width, width), BF16)],
+        2 * tok_rows * width * width,
+        place,
+        own,
+        rows_in,
+        bias,
+        gain,
+        shift,
+        *parts,
+        *weights,
+    )
+
+
+GELU_SLOPE = math.sqrt(2 / math.pi)
+GELU_CUBE = 0.044715
+
+
+def feed_kernel(
+    first_ref,
+    second_ref,
+    first_grad_ref,
+    second_grad_ref,
+    up_ref,
+    bias_ref,
+    down_ref,
+    act_ref,
+    pre_ref,
+    first_back_ref,
+    second_back_ref,
+    first_out_ref,
+    second_out_ref,
+    shift_ref,
+):
+    tok_rows = first_ref.shape[0]
+    sums = 0.0
+    for at, rows_ref, grads_ref, back_ref, out_ref in (
+        (0, first_ref, first_grad_ref, first_back_ref, first_out_ref),
+        (tok_rows, second_ref, second_grad_ref, second_back_ref, second_out_ref),
+    ):
+        rows = pl.ds(at, tok_rows)
+        hidden = dot_nn(rows_ref[...], up_ref[...]) + bias_ref[...]
+        square = hidden * hidden
+        turn = jnp.tanh(hidden * (GELU_SLOPE + GELU_SLOPE * GELU_CUBE * square))
+        half = 0.5 + 0.5 * turn
+        act = (hidden * half).astype(BF16)
+        act_ref[rows, :] = act
+        slope = half + 0.5 * hidden * (1.0 - turn * turn) * (
+            GELU_SLOPE + 3 * GELU_SLOPE * GELU_CUBE * square
+        )
+        pre = (dot_nt(grads_ref[...], down_ref[...]) * slope).astype(BF16)
+        pre_ref[rows, :] = pre
+        sums = sums + jnp.sum(pre.astype(F32), axis=0, keepdims=True)
+        back_ref[...] = dot_nt(pre, up_ref[...]).astype(back_ref.dtype)
+        out_ref[...] = dot_nn(act, down_ref[...]).astype(out_ref.dtype)
+    shift_ref[...] = sums
+
+
+def feed_forward(place, first, second, first_grad, second_grad, up, bias, down, first_type, name):
+    tok_rows, width = first.shape
+    units = up.shape[1]
+
+    def kernel(place_ref, *refs):
+        feed_kernel(*refs)
+
+    return whole_call(
+        kernel,
+        name,
+        [
+            jax.ShapeDtypeStruct((2 * tok_rows, units), BF16),
+            jax.ShapeDtypeStruct((2 * tok_rows, units), BF16),
+            jax.ShapeDtypeStruct((tok_rows, width), first_type),
+            jax.ShapeDtypeStruct((tok_rows, width), BF16),
+            jax.ShapeDtypeStruct((tok_rows, width), first_type),
+            jax.ShapeDtypeStruct((tok_rows, width), BF16),
+            jax.ShapeDtypeStruct((1, units), F32),
+        ],
+        [],
+        16 * tok_rows * width * units,
+        place,
+        first,
+        second,
+        first_grad,
+        second_grad,
+        up,
+        bias,
+        down,
+    )
+
+
+def residual_back_kernel(
+    n_ctx, n_wsh, place_ref, own_ref, near_ref, far_ref, residual_ref, cotangent_ref, gain_ref, *refs
+):
+    weights, refs = refs[:n_wsh], refs[n_wsh:]
+    total_ref, low_ref, sum_gain_ref, sum_shift_ref, sum_low_ref, *refs = refs
+    sends, (weight_ref,) = refs[:n_ctx], refs[n_ctx:]
+    ctx, wsh = place_ref[0], place_ref[1]
+    weight_rows = weights[0].shape[0]
+    for k in range(n_wsh):
+        at = pl.multiple_of((wsh ^ k) * weight_rows, 16)
+        weight_ref[pl.ds(at, weight_rows), :] = weights[k][...]
+    grad = own_ref[...] + near_ref[...].astype(F32) + far_ref[...].astype(F32)
+    centre, inverse = centred(residual_ref[...])
+    unit = centre * inverse
+    sum_gain_ref[...] = jnp.sum(grad * unit, axis=0, keepdims=True)
+    sum_shift_ref[...] = jnp.sum(grad, axis=0, keepdims=True)
+    total = cotangent_ref[...].astype(F32) + norm_back(unit, inverse, grad * gain_ref[...])
+    total_ref[...] = total
+    low = total.astype(BF16)
+    low_ref[...] = low
+    sum_low_ref[...] = jnp.sum(low.astype(F32), axis=0, keepdims=True)
+    shared = dot_nt(low, weight_ref[pl.ds(n_ctx * LANES, HD), :])
+    shared = jnp.concatenate([shared, jnp.zeros_like(shared)], axis=1).astype(BF16)
+    for j in range(n_ctx):
+        at = pl.multiple_of((ctx ^ j) * LANES, LANES)
+        sends[j][:, pl.ds(0, LANES)] = dot_nt(low, weight_ref[pl.ds(at, LANES), :]).astype(BF16)
+        sends[j][:, pl.ds(LANES, LANES)] = shared
+
+
+def residual_back(place, own, near, far, residual, cotangent, gain, weights, n_ctx):
+    tok_rows, width = residual.shape
+    row = jax.ShapeDtypeStruct((1, width), F32)
+    out = whole_call(
+        functools.partial(residual_back_kernel, n_ctx, len(weights)),
+        "residual_back",
+        [
+            jax.ShapeDtypeStruct((tok_rows, width), F32),
+            jax.ShapeDtypeStruct((tok_rows, width), BF16),
+            row,
+            row,
+            row,
+        ]
+        + [jax.ShapeDtypeStruct((tok_rows, 2 * LANES), BF16)] * n_ctx,
+        [pltpu.VMEM((width, width), BF16)],
+        2 * tok_rows * width * width,
+        place,
+        own,
+        near,
+        far,
+        residual,
+        cotangent,
+        gain,
+        *weights,
+    )
+    total, low, sum_gain, sum_shift, sum_low, *sends = out
+    return total, low, sum_gain, sum_shift, sum_low, sends
+
+
+def input_back_kernel(n_ctx, n_wsh, place_ref, own_ref, in_ref, total_ref, gain_ref, *refs):
+    parts, refs = refs[:n_ctx], refs[n_ctx:]
+    weights, refs = refs[:n_wsh], refs[n_wsh:]
+    back_ref, sum_gain_ref, sum_shift_ref, weight_ref, grad_ref = refs
+    ctx, wsh = place_ref[0], place_ref[1]
+    weight_rows = weights[0].shape[0] // 3
+    grad = 0.0
+    for part in range(3):
+        for k in range(n_wsh):
+            at = pl.multiple_of((wsh ^ k) * weight_rows, 16)
+            rows = pl.ds(part * weight_rows, weight_rows)
+            weight_ref[pl.ds(at, weight_rows), :] = weights[k][rows, :]
+        for j in range(n_ctx):
+            at = pl.multiple_of((ctx ^ j) * LANES, LANES)
+            grad_ref[:, pl.ds(at, LANES)] = parts[j][:, pl.ds(part * LANES, LANES)]
+        grad_ref[:, pl.ds(n_ctx * LANES, HD)] = own_ref[:, pl.ds(part * LANES, HD)]
+        grad = grad + dot_nt(grad_ref[...], weight_ref[...])
+    centre, inverse = centred(in_ref[...].astype(F32))
+    unit = centre * inverse
+    sum_gain_ref[...] = jnp.sum(grad * unit, axis=0, keepdims=True)
+    sum_shift_ref[...] = jnp.sum(grad, axis=0, keepdims=True)
+    total = total_ref[...] + norm_back(unit, inverse, grad * gain_ref[...])
+    back_ref[...] = total.astype(BF16)
+
+
+def input_back(place, own, rows_in, total, gain, parts, weights):
+    tok_rows, width = rows_in.shape
+    row = jax.ShapeDtypeStruct((1, width), F32)
+    return whole_call(
+        functools.partial(input_back_kernel, len(parts), len(weights)),
+        "input_back",
+        [jax.ShapeDtypeStruct((tok_rows, width), BF16), row, row],
+        [pltpu.VMEM((width, width), BF16), pltpu.VMEM((tok_rows, width), BF16)],
+        6 * tok_rows * width * width,
+        place,
+        own,
+        rows_in,
+        total,
+        gain,
+        *parts,
+        *weights,
+    )
+
+
+def lay_rows_kernel(place_ref, *refs):
+    *parts, out_ref = refs
+    rows = parts[0].shape[0]
+    for j, part in enumerate(parts):
+        at = pl.multiple_of((place_ref[0] ^ j) * rows, 8)
+        out_ref[pl.ds(at, rows), :] = part[...].astype(F32)
+
+
+def lay_rows(place, parts):
+    rows, columns = parts[0].shape
+    shape = jax.ShapeDtypeStruct((rows * len(parts), columns), F32)
+    return whole_call(lay_rows_kernel, "lay_rows", [shape], [], 0, place, *parts)[0]
+
+
+def lay_qkv_kernel(place_ref, own_ref, *refs):
+    *parts, out_ref, row_ref = refs
+    n_ctx = len(parts)
+    width = row_ref.shape[1]
+    for kind in range(3):
+        for j, part in enumerate(parts):
+            at = pl.multiple_of((place_ref[0] ^ j) * LANES, LANES)
+            row_ref[:, pl.ds(at, LANES)] = part[:, pl.ds(kind * LANES, LANES)].astype(F32)
+        shared = own_ref[:, pl.ds(kind * LANES, LANES)].astype(F32)
+        row_ref[:, pl.ds(n_ctx * LANES, HD)] = shared[:, :HD]
+        out_ref[:, pl.ds(kind * width, width)] = row_ref[...]
+
+
+def lay_qkv(place, own, parts, width):
+    rows = own.shape[0]
+    shape = jax.ShapeDtypeStruct((rows, 3 * width), F32)
+    scratch = [pltpu.VMEM((rows, width), F32)]
+    return whole_call(lay_qkv_kernel, "lay_qkv", [shape], scratch, 0, place, own, *parts)[0]
+
+
+def gather_wsh(block):
+    across = swap(block, "wsh", 2)
+    return [block, swap(block, "wsh", 1), across, swap(across, "wsh", 1)]
+
+
+def gather_ctx(block):
+    far = [block] + [swap(block, "ctx", j) for j in (2, 4, 6)]
+    near = [swap(part, "ctx", 1) for part in far]
+    return [part for pair in zip(far, near) for part in pair]
+
+
+def ordered(parts, mine):
+    return [
+        sum(jnp.where(mine ^ k == i, part, jnp.zeros_like(part)) for k, part in enumerate(parts))
+        for i in range(len(parts))
+    ]
+
+
+def pick(pieces, index, axis=0):
+    return lax.dynamic_index_in_dim(pieces, index, axis, keepdims=False)
+
+
+def scatter_ctx(grad, ctx):
+    rows, columns = grad.shape
+    near, far = ctx & 1, ctx >> 1
+    pieces = grad.reshape(4, 2, rows // 8, columns)
+    kept = pick(pieces, near, 1)
+    half = kept + swap(pick(pieces, 1 - near, 1).astype(BF16), "ctx", 1).astype(F32)
+    total = pick(half, far)
+    for k in range(1, 4):
+        total = total + swap(pick(half, far ^ k).astype(BF16), "ctx", 2 * k).astype(F32)
+    return total.astype(BF16)
+
+
+def sum_over(value, axis):
+    distance = 1
+    while distance < lax.axis_size(axis):
+        value = value + swap(value, axis, distance)
+        distance *= 2
+    return value
+
+
+def by_heads(
+    block_in,
+    doc_flags,
+    ln1_gain,
+    ln1_bias,
+    w_qkv,
+    qv_bias,
+    w_out,
+    out_bias,
+    ln2_gain,
+    ln2_bias,
+    w_up,
+    up_bias,
+    w_down,
+    down_bias,
+    cotangent,
+):
+    n_ctx, n_wsh = lax.axis_size("ctx"), lax.axis_size("wsh")
+    ctx, wsh = lax.axis_index("ctx"), lax.axis_index("wsh")
+    place = jnp.stack([ctx, wsh]).astype(jnp.int32)
+    tok_rows, width = block_in.shape[1:]
+    length = n_ctx * tok_rows
+    shard = ln1_gain.shape[0]
+    rows_in, rows_grad = block_in[0], cotangent[0]
+
+    blocks = gather_ctx(rows_in)
+    columns = []
+    for kind in range(3):
+        pair = lax.dynamic_slice_in_dim(w_qkv, kind * width + ctx * LANES, LANES, 1)
+        shared = w_qkv[:, (kind + 1) * width - HD : (kind + 1) * width]
+        columns += [pair, shared, jnp.zeros((shard, LANES - HD), BF16)]
+    weight_parts = gather_wsh(jnp.concatenate(columns, axis=1))
+
+    packed = jnp.concatenate([ln1_gain, ln1_bias, qv_bias, out_bias, ln2_gain, ln2_bias, down_bias])
+    packed = jnp.stack(ordered(gather_wsh(packed), wsh)).astype(F32)
+
+    def vector(at, size):
+        return packed[:, at * shard : at * shard + size].reshape(1, n_wsh * size)
+
+    gain_one, shift_one, qv_full = vector(0, shard), vector(1, shard), vector(2, 2 * shard)
+    out_shift, gain_two, shift_two, down_shift = [vector(at, shard) for at in (4, 5, 6, 7)]
+    gap = jnp.zeros((1, LANES - HD), F32)
+    query_shift = lax.dynamic_slice_in_dim(qv_full, ctx * LANES, LANES, 1)
+    value_shift = lax.dynamic_slice_in_dim(qv_full, width + ctx * LANES, LANES, 1)
+    head_shift = jnp.concatenate(
+        [
+            query_shift,
+            qv_full[:, width - HD : width],
+            gap,
+            jnp.zeros((1, 2 * LANES), F32),
+            value_shift,
+            qv_full[:, 2 * width - HD :],
+            gap,
+        ],
+        axis=1,
+    )
+
+    flags = doc_flags
+    for distance in (1, 2, 4):
+        flags = jnp.concatenate([flags, swap(flags, "ctx", distance)], axis=0)
+    flags = jnp.concatenate(ordered([flags[j : j + 1] for j in range(n_ctx)], ctx), axis=1)
+    places = jnp.arange(length, dtype=jnp.int32)
+    started = jnp.where(flags[0] == 1, places, 0)
+    start_row = jnp.max(
+        jnp.where(places[:, None] <= places[None, :], started[:, None], 0), axis=0, keepdims=True
+    )
+
+    out_parts = gather_wsh(w_out)
+    grads = gather_wsh(rows_grad)
+    qkv_rows = jnp.concatenate([w_qkv[:, k * width : (k + 1) * width] for k in range(3)], axis=0)
+
+    normed_one, qkv, attended, log_total, own_low, sends = attend_forward(
+        place, start_row, gain_one, shift_one, head_shift, blocks, weight_parts
+    )
+    parts = [sends[0]] + [swap(sends[j], "ctx", j) for j in range(1, n_ctx)]
+    attended_low, residual, normed_two, branch_squares = out_project(
+        place, own_low, rows_in, out_shift, gain_two, shift_two, parts, out_parts
+    )
+    normed_parts = gather_wsh(normed_two)
+    unit_shift = up_bias.astype(F32).reshape(1, -1)
+    act_near, pre_near, back_0, back_1, out_0, out_1, up_sum_near = feed_forward(
+        place,
+        normed_parts[0],
+        normed_parts[1],
+        grads[0],
+        grads[1],
+        w_up,
+        unit_shift,
+        w_down,
+        F32,
+        "feed_near",
+    )
+    act_far, pre_far, back_2, back_3, out_2, out_3, up_sum_far = feed_forward(
+        place,
+        normed_parts[2],
+        normed_parts[3],
+        grads[2],
+        grads[3],
+        w_up,
+        unit_shift,
+        w_down,
+        F32,
+        "feed_far",
+    )
+
+    def to_streams(part_1, part_2, part_3):
+        near = swap(part_1, "wsh", 1)
+        across = part_2 + swap(part_3, "wsh", 1).astype(F32)
+        return near, swap(across.astype(BF16), "wsh", 2)
+
+    back_near, back_across = to_streams(back_1, back_2, back_3)
+    residual_grad, attn_grad, sum_gain_two, sum_shift_two, sum_attn, grad_sends = residual_back(
+        place, back_0, back_near, back_across, residual, rows_grad, gain_two, out_parts, n_ctx
+    )
+    grad_parts = [grad_sends[0]] + [swap(grad_sends[j], "ctx", j) for j in range(1, n_ctx)]
+    qkv_grad, own_grad, qkv_sends = attend_backward(
+        place, start_row, qkv, attended, log_total, grad_parts
+    )
+    qkv_parts = [qkv_sends[0]] + [swap(qkv_sends[j], "ctx", j) for j in range(1, n_ctx)]
+    weight_full = gather_wsh(qkv_rows)
+    input_grad, sum_gain_one, sum_shift_one = input_back(
+        place, own_grad, rows_in, residual_grad, gain_one, qkv_parts, weight_full
+    )
+
+    out_near, out_across = to_streams(out_1, out_2, out_3)
+    mlp_branch = out_0 + out_near.astype(F32) + out_across.astype(F32) + down_shift
+    block_full = residual + mlp_branch
+    squares = jnp.stack(
+        [jnp.sum(branch_squares), jnp.sum(mlp_branch * mlp_branch), jnp.sum(block_full * block_full)]
+    )
+
+    act = jnp.concatenate([act_near, act_far], axis=0)
+    pre = jnp.concatenate([pre_near, pre_far], axis=0)
+    rows_two = jnp.concatenate(normed_parts, axis=0)
+    all_grads = jnp.concatenate(grads, axis=0)
+    grad_down = lay_rows(place, gather_ctx(scatter_ctx(dot_tn(act, all_grads), ctx)))
+    grad_up = lay_rows(place, gather_ctx(scatter_ctx(dot_tn(rows_two, pre), ctx)))
+
+    def scatter_wsh(grad):
+        pieces = grad.reshape(n_wsh, grad.shape[0] // n_wsh, grad.shape[1])
+        part = [pick(pieces, wsh ^ k) for k in range(n_wsh)]
+        near, across = to_streams(part[1].astype(BF16), part[2], part[3].astype(BF16))
+        return part[0] + near.astype(F32) + across.astype(F32)
+
+    out_piece = scatter_wsh(dot_tn(attended_low, attn_grad))
+    out_piece = jnp.pad(out_piece, ((0, 112), (0, 0)))
+    grad_out = lay_rows(place, gather_ctx(scatter_ctx(out_piece, ctx)))[:shard]
+    head_grad = scatter_wsh(dot_tn(normed_one, qkv_grad)).astype(BF16)
+    pair_grad = jnp.concatenate([head_grad[:, 2 * k * LANES : (2 * k + 1) * LANES] for k in range(3)], 1)
+    own_piece = jnp.concatenate(
+        [head_grad[:, (2 * k + 1) * LANES : (2 * k + 2) * LANES] for k in range(3)], 1
+    )
+    grad_qkv = lay_qkv(place, own_piece, gather_ctx(pair_grad), width)
+
+    head_sums = jnp.sum(qkv_grad.astype(F32), axis=0, keepdims=True)
+    first = jnp.where(ctx == 0, 1.0, 0.0)
+    qv_sum = jnp.zeros((1, 2 * width), F32)
+    for kind, at in ((0, 0), (2, width)):
+        pair = head_sums[:, 2 * kind * LANES : (2 * kind + 1) * LANES]
+        shared = head_sums[:, (2 * kind + 1) * LANES : (2 * kind + 1) * LANES + HD]
+        qv_sum = lax.dynamic_update_slice(qv_sum, pair, (0, at + ctx * LANES))
+        qv_sum = lax.dynamic_update_slice(qv_sum, shared * first, (0, at + n_ctx * LANES))
+    sum_down = jnp.sum(rows_grad.astype(F32), axis=0, keepdims=True)
+    early = jnp.concatenate([sum_gain_two, sum_shift_two, sum_attn, sum_down], axis=1)
+    along = jnp.concatenate([early, up_sum_near + up_sum_far, squares.reshape(1, 3)], axis=1)
+    along = sum_over(along, "ctx")
+    early = sum_over(along[:, : 4 * width], "wsh")
+    up_sum = along[0, 4 * width : 4 * width + up_bias.shape[0]]
+    rms_values = jnp.sqrt(along[:, -3:] / (length * width))
+    late = jnp.concatenate([sum_gain_one, sum_shift_one, qv_sum], axis=1)
+    late = sum_over(sum_over(late, "ctx"), "wsh")
+
+    def mine(vectors, at, size=shard):
+        return lax.dynamic_slice_in_dim(vectors[0], at * width + wsh * size, size)
+
+    return (
+        block_full.astype(BF16)[None],
+        input_grad[None],
+        mine(late, 0),
+        mine(late, 1),
+        grad_qkv,
+        mine(late, 2, 2 * shard),
+        grad_out,
+        mine(early, 2),
+        mine(early, 0),
+        mine(early, 1),
+        grad_up,
+        up_sum,
+        grad_down,
+        mine(early, 3),
+        rms_values,
+    )
 
 
 def prefix(shard, axis, combine, identity):
@@ -64,7 +823,7 @@
     )
 
 
-def local(
+def by_tokens(
     block_in,
     doc_flags,
     ln1_gain,
@@ -85,7 +844,10 @@
     model_width = block_in.shape[2]
     scaling = HD ** (-0.5)
     ctx_count = lax.axis_size("ctx")
-    running_count = jnp.cumsum(doc_flags[0])
+    earlier = jnp.arange(tok_rows)
+    running_count = jnp.sum(
+        jnp.where(earlier[None, :] <= earlier[:, None], doc_flags[0][None, :], 0), axis=1
+    )
     offset_count = prefix(running_count[-1], "ctx", add_counts, jnp.int32(0))
     local_segment = running_count + offset_count - 1
     local_place = lax.axis_index("ctx") * tok_rows + jnp.arange(tok_rows, dtype=jnp.int32)
@@ -344,8 +1106,10 @@
 
 
 def solution(mesh):
+    each = LANES // HD
+    by_head = mesh.shape["ctx"] == 8 and mesh.shape["ctx"] * each + 1 == H and mesh.shape["wsh"] == 4
     return jax.shard_map(
-        local,
+        by_heads if by_head else by_tokens,
         mesh=mesh,
         in_specs=(
             P("wsh", "ctx", None),

time: 1320 us -> 504 us (0.38)
  blocking collectives: 699 us -> 0 us
  waiting for transfers between devices: 419 us -> 170 us
  starting transfers between devices: 0.95 us -> 152 us
  matrix products: 112 us -> 24.8 us
  Pallas kernels: 0 us -> 71.1 us
  between operations: 19.1 us -> 2.45 us
    psum x1 -> x0, blocking collectives: 574 us -> none  [local(): lax.psum((sum_gain_one, sum_shift_one, sum_qkv, sum_qv_shift, sum_out, su...]
    all_gather x8 -> x0, waiting for transfers between devices: 224 us -> none  [the longest x1 64.6 us: local(): lax.all_gather(w_up, 'wsh', axis=1, tiled=True)]
    ppermute x0 -> x111, waiting for transfers between devices: none -> 170 us  [swap(): return lax.ppermute(value, axis, [(i, i ^ distance) for i in range(size)])]
    ppermute x0 -> x111, starting transfers between devices: none -> 152 us  [swap(): return lax.ppermute(value, axis, [(i, i ^ distance) for i in range(size)])]
    reduce_scatter x3 -> x0, waiting for transfers between devices: 107 us -> none  [the longest x1 80.6 us: local(): lax.psum_scatter(grad_down.astype(jnp.bfloat16), 'wsh', scatter_dimension...]
    all_gather x4 -> x0, blocking collectives: 97.1 us -> none  [the longest x1 32.7 us: local(): segment_piece = lax.all_gather(local_segment, 'ctx', axis=0, tiled=True)]
    unnamed x13 -> x0, waiting for transfers between devices: 87.5 us -> none
    dot_general x18 -> x4, matrix products: 112 us -> 24.8 us  [dot_tn(): lax.dot_general(left, right, (((0,), (0,)), ((), ())), preferred_element_...]
  transfers between devices with their start and end apart: 12 -> 111, of which waited for: 9 -> 30; matrix products, arithmetic and copies ran while one was open for 12% -> 17% of each run, Pallas kernels for 0% -> 13%
where the time goes in v1:
time: 504 us; the launch traced here: 494 us
  waiting for transfers between devices  170 us (34%)
  starting transfers between devices  152 us (30%)
  Pallas kernels  71.1 us (14%)
  local copies, waits for them, and re-layouts  47.1 us (9%)
  other arithmetic  26.8 us (5%)
  matrix products  24.8 us (5%)
    ppermute x111, waiting for transfers between devices, swap(): return lax.ppermute(value, axis, [(i, i ^ distance) for i in range(size)])  170 us
    ppermute x111, starting transfers between devices, swap(): return lax.ppermute(value, axis, [(i, i ^ distance) for i in range(size)])  152 us
    pallas_call x9, Pallas kernels, whole_call(): pl.pallas_call(kernel, out_shape=shapes, in_specs=[pl.BlockSpec(memory_sp...  49 us
    dot_general x4, matrix products, dot_tn(): lax.dot_general(left, right, (((0,), (0,)), ((), ())), preferred_element_...  24.8 us
    pallas_call x1, Pallas kernels, attend_forward(): pl.pallas_call(functools.partial(attend_forward_kernel, n_ctx, n_wsh), ou...  11.6 us
    unnamed x200, local copies, waits for them, and re-layouts  10.8 us
    pallas_call x1, Pallas kernels, attend_backward(): pl.pallas_call(functools.partial(attend_backward_kernel, n_ctx), out_shap...  10.6 us
  transfers between devices with their start and end apart: 111, of which 30 were waited for; matrix products, arithmetic and copies ran while one was open for 17% of the time, Pallas kernels for 13%

profile of v1, /device:TPU:0, one launch (start us, length us, event | category | flops | bytes accessed | tf_op | source)
XLA Modules:
  0.0 494.1 jit_solution(5978672228986175770)
XLA Ops:
  0.7 5.0 %concatenate.49 = bf16[2176]{0:T(1024)(128)(2,1)S(1)} concatenate(bf16[272]{0:T(512)(128)(2,1)} %param.17, bf16[272]{0:T(512)(128)(2,1)} %param.18, bf16[544]{0:T(1024)(128)(2,1)} %param.20, bf16[272]{0:T(512)(128)(2,1)} %param.22, bf16[272]{0:T(512)(128)(2,1)} %param.23, bf16[272]{0:T(512)(128)(2,1)} %param.24, bf16[272]{0:T(512)(128)(2,1)} %param.28), dimensions={0} | concatenate | bytes 8704 | tf_op jit(solution)/shard_map/concatenate | solution.py:612
  5.6 3.0 collective-permute-start.4
  16.4 3.0 collective-permute-done
  24.3 2.6 collective-permute-start.2
  28.8 2.6 collective-permute-start.9
  36.4 13.6 %collective-permute-done.9.refs_4_ = bf16[128,1088]{1,0:T(8,128)(2,1)} collective-permute-done((bf16[128,1088]{1,0:T(8,128)(2,1)S(1)}, bf16[128,1088]{1,0:T(8,128)(2,1)}, u32[]{:S(2)}, u32[]{:S(2)}) %collective-permute-start.9) | collective-permute-done | bytes 278560 | tf_op jit(solution)/shard_map/ppermute | solution.py:38
  56.1 6.0 %collective-permute-done.10.refs_5_ = bf16[128,1088]{1,0:T(8,128)(2,1)} collective-permute-done((bf16[128,1088]{1,0:T(8,128)(2,1)}, bf16[128,1088]{1,0:T(8,128)(2,1)}, u32[]{:S(2)}, u32[]{:S(2)}) %collective-permute-start.10) | collective-permute-done | bytes 278560 | tf_op jit(solution)/shard_map/ppermute | solution.py:38
  62.1 5.5 %collective-permute-done.12.refs_7_ = bf16[128,1088]{1,0:T(8,128)(2,1)} collective-permute-done((bf16[128,1088]{1,0:T(8,128)(2,1)}, bf16[128,1088]{1,0:T(8,128)(2,1)}, u32[]{:S(2)}, u32[]{:S(2)}) %collective-permute-start.12) | collective-permute-done | bytes 278560 | tf_op jit(solution)/shard_map/ppermute | solution.py:38
  67.6 11.6 %attend_forward.1 = (bf16[1024,1088]{1,0:T(8,128)(2,1)}, bf16[1024,768]{1,0:T(8,128)(2,1)}, f32[192,1024]{1,0:T(8,128)}, f32[8,1024]{1,0:T(8,128)}, bf16[128,128...) custom-call(s32[2]{0:T(128)} %pad_add_fusion.2.place_ref, ...), custom_call_target="tpu_custom_call" | custom-call | flops 2516582400 | bytes 7700480 | tf_op jit(solution)/shard_map/attend_forward/pallas_call | solution.py:150
  80.7 4.2 collective-permute-start.17
  85.1 4.0 collective-permute-start.19
  100.6 3.9 out_project.1
  107.6 6.7 %collective-permute-done.29.refs_0_ = bf16[128,1088]{1,0:T(8,128)(2,1)} collective-permute-done((bf16[128,1088]{1,0:T(8,128)(2,1)}, bf16[128,1088]{1,0:T(8,128)(2,1)}, u32[]{:S(2)}, u32[]{:S(2)}) %collective-permute-start.29) | collective-permute-done | bytes 278560 | tf_op jit(solution)/shard_map/ppermute | solution.py:38
  115.7 8.6 %feed_near.1 = (bf16[256,1088]{1,0:T(8,128)(2,1)}, bf16[256,1088]{1,0:T(8,128)(2,1)}, f32[128,1088]{1,0:T(8,128)}, bf16[128,1088]{1,0:T(8,128)(2,1)}, f32[128,10...) custom-call(s32[2]{0:T(128)} %pad_add_fusion.2.place_ref, bf16[128,1088]{1,0:T(8,128)(2,1)} %get-tuple-element.82.refs_0_, ...), custom_call_target="tpu_custom_call" | custom-call | flops 2424307712 | bytes 8643072 | tf_op jit(solution)/shard_map/feed_near/pallas_call | solution.py:288
  126.4 8.7 %feed_far.1 = (bf16[256,1088]{1,0:T(8,128)(2,1)}, bf16[256,1088]{1,0:T(8,128)(2,1)}, f32[128,1088]{1,0:T(8,128)}, bf16[128,1088]{1,0:T(8,128)(2,1)}, f32[128,108...) custom-call(s32[2]{0:T(128)} %pad_add_fusion.2.place_ref, ...), custom_call_target="tpu_custom_call" | custom-call | flops 2424307712 | bytes 8643072 | tf_op jit(solution)/shard_map/feed_far/pallas_call | solution.py:288
  136.3 3.1 fusion.4
  139.5 16.5 %fusion.15 = f32[1088,1088]{1,0:T(8,128)} fusion(bf16[256,1088]{1,0:T(8,128)(2,1)S(1)} %copy-done.96, bf16[256,1088]{1,0:T(8,128)(2,1)S(1)} %copy-done.95, bf16[128,1088]{1,0:T(8,128)(2,1)S(1)} %copy-done.79, bf16[128,1088]{1,0:T(8,128)(2,1)} %collective-permute-done.31.refs_2_, bf16[128,1088]{1,0:T(8,128)(2,1)} %collective-permute-done.27.refs_3_, ...), kind=kOutput, calls=%fused_computation.27 | convolution fusion | flops 1218838528 | bytes 6963200 | tf_op jit(solution)/shard_map/dot_general | solution.py:33
  159.5 7.6 %collective-permute-done.34 = bf16[128,1088]{1,0:T(8,128)(2,1)S(1)} collective-permute-done((bf16[128,1088]{1,0:T(8,128)(2,1)S(1)}, bf16[128,1088]{1,0:T(8,128)(2,1)S(1)}, u32[]{:S(2)}, u32[]{:S(2)}) %collective-permute-start.34) | collective-permute-done | bytes 278560 | tf_op jit(solution)/shard_map/ppermute | solution.py:38
  170.0 2.9 collective-permute-done.37.far_ref
  173.7 4.6 residual_back.1
  180.8 2.9 fusion.1
  206.1 10.6 %attend_backward.1 = (bf16[1024,768]{1,0:T(8,128)(2,1)}, bf16[128,384]{1,0:T(8,128)(2,1)}, bf16[128,384]{1,0:T(8,128)(2,1)}, bf16[128,384]{1,0:T(8,128)(2,1)}, b...) custom-call(s32[2]{0:T(128)} %pad_add_fusion.2.place_ref, ...), custom_call_target="tpu_custom_call" | custom-call | flops 2013265920 | bytes 5242880 | tf_op jit(solution)/shard_map/attend_backward/pallas_call | solution.py:238
  219.5 3.4 fusion.124
  231.3 15.2 %collective-permute-done.53.refs_10_ = bf16[816,1088]{1,0:T(8,128)(2,1)} collective-permute-done((bf16[816,1088]{1,0:T(8,128)(2,1)S(1)}, bf16[816,1088]{1,0:T(8,128)(2,1)}, u32[]{:S(2)}, u32[]{:S(2)}) %collective-permute-start.53) | collective-permute-done | bytes 1775648 | tf_op jit(solution)/shard_map/ppermute | solution.py:38
  249.9 2.5 fusion.2
  254.6 22.4 %collective-permute-done.100 = bf16[4,136,1088]{2,1,0:T(8,128)(2,1)S(1)} collective-permute-done((bf16[4,136,1088]{2,1,0:T(8,128)(2,1)}, bf16[4,136,1088]{2,1,0:T(8,128)(2,1)S(1)}, u32[]{:S(2)}, u32[]{:S(2)}) %collective-permute-start.100) | collective-permute-done | bytes 1183776 | tf_op jit(solution)/shard_map/ppermute | solution.py:38
  287.7 2.4 collective-permute-start.49
  291.9 2.7 collective-permute-start.51
  297.5 3.5 collective-permute-done.49.refs_5_
  303.2 2.7 collective-permute-start.91
  305.9 11.4 %collective-permute-start.90 = (bf16[136,1088]{1,0:T(8,128)(2,1)}, bf16[136,1088]{1,0:T(8,128)(2,1)}, u32[]{:S(2)}, u32[]{:S(2)}) collective-permute-start(bf16[136,1088]{1,0:T(8,128)(2,1)} %get-tuple-element.190), channel_id=1, source_target_pairs={{0,8},{4,12},{8,0},{12,4},{16,24},{20,28},{24,16},{28,20},{1,9},{5... | collective-permute-start | bytes 887816 | tf_op jit(solution)/shard_map/ppermute | solution.py:38
  318.5 7.9 %input_back.1 = (bf16[128,1088]{1,0:T(8,128)(2,1)}, f32[1,1088]{1,0:T(1,128)}, f32[1,1088]{1,0:T(1,128)}) custom-call(s32[2]{0:T(128)} %pad_add_fusion.2.place_ref, bf16[128,384]{1,0:T(8,128)(2,1)} %get-tuple-element.102.own_ref, bf16[128,1088]{1,0:T(8,128)(2,1)} %bitcast.135, f32[128,1088]{1,0:T(8,128)} %get-tuple-element.103.total_ref, ...), custom_call_target="tpu_custom_call" | custom-call | flops 909115392 | bytes 9114368 | tf_op jit(solution)/shard_map/input_back/pallas_call | solution.py:288
  337.7 6.7 %collective-permute-done.56 = f32[1,4352]{1,0:T(1,128)S(1)} collective-permute-done((f32[1,4352]{1,0:T(1,128)S(1)}, f32[1,4352]{1,0:T(1,128)S(1)}, u32[]{:S(2)}, u32[]{:S(2)}) %collective-permute-start.56) | collective-permute-done | bytes 17440 | tf_op jit(solution)/shard_map/ppermute | solution.py:38
  347.0 2.9 collective-permute-start.57
  351.6 6.6 %collective-permute-done.57 = f32[1,4352]{1,0:T(1,128)S(1)} collective-permute-done((f32[1,4352]{1,0:T(1,128)S(1)}, f32[1,4352]{1,0:T(1,128)S(1)}, u32[]{:S(2)}, u32[]{:S(2)}) %collective-permute-start.57) | collective-permute-done | bytes 17440 | tf_op jit(solution)/shard_map/ppermute | solution.py:38
  367.6 8.1 %collective-permute-done.66.refs_4_ = bf16[272,384]{1,0:T(8,128)(2,1)S(1)} collective-permute-done((bf16[272,384]{1,0:T(8,128)(2,1)S(1)}, bf16[272,384]{1,0:T(8,128)(2,1)S(1)}, u32[]{:S(2)}, u32[]{:S(2)}) %collective-permute-start.66) | collective-permute-done | bytes 208928 | tf_op jit(solution)/shard_map/ppermute | solution.py:38
  381.3 13.8 %collective-permute-start.105 = (bf16[136,1088]{1,0:T(8,128)(2,1)S(1)}, bf16[136,1088]{1,0:T(8,128)(2,1)S(1)}, u32[]{:S(2)}, u32[]{:S(2)}) collective-permute-start(bf16[136,1088]{1,0:T(8,128)(2,1)S(1)} %fusion.33.refs_0_), channel_id=1, source_target_pairs={{0,8},{4,12},{8,0},{12,4},{16,24},{20,28},{24,16},{28,20},{1,9},{5... | collective-permute-start | bytes 887816 | tf_op jit(solution)/shard_map/ppermute | solution.py:38
  395.1 6.2 %collective-permute-done.96.refs_4_ = bf16[136,1088]{1,0:T(8,128)(2,1)S(1)} collective-permute-done((bf16[136,1088]{1,0:T(8,128)(2,1)S(1)}, bf16[136,1088]{1,0:T(8,128)(2,1)S(1)}, u32[]{:S(2)}, u32[]{:S(2)}) %collective-permute-start.96) | collective-permute-done | bytes 295968 | tf_op jit(solution)/shard_map/ppermute | solution.py:38
  406.9 20.3 %collective-permute-done.107.refs_4_ = bf16[136,1088]{1,0:T(8,128)(2,1)S(1)} collective-permute-done((bf16[136,1088]{1,0:T(8,128)(2,1)S(1)}, bf16[136,1088]{1,0:T(8,128)(2,1)S(1)}, u32[]{:S(2)}, u32[]{:S(2)}) %collective-permute-start.107) | collective-permute-done | bytes 295968 | tf_op jit(solution)/shard_map/ppermute | solution.py:38
  431.1 5.0 %collective-permute-start.75 = (bf16[48,1088]{1,0:T(8,128)(2,1)S(1)}, bf16[48,1088]{1,0:T(8,128)(2,1)S(1)}, u32[]{:S(2)}, u32[]{:S(2)}) collective-permute-start(bf16[48,1088]{1,0:T(8,128)(2,1)S(1)} %get-tuple-element.204), channel_id=1, source_target_pairs={{0,16},{4,20},{8,24},{12,28},{16,0},{20,4},{24,8},{28,12},{1,17},{... | collective-permute-start | bytes 313352 | tf_op jit(solution)/shard_map/ppermute | solution.py:38
  445.0 3.8 collective-permute-done.97.refs_5_
  449.7 5.8 %collective-permute-done.99.refs_7_ = bf16[136,1088]{1,0:T(8,128)(2,1)S(1)} collective-permute-done((bf16[136,1088]{1,0:T(8,128)(2,1)S(1)}, bf16[136,1088]{1,0:T(8,128)(2,1)S(1)}, u32[]{:S(2)}, u32[]{:S(2)}) %collective-permute-start.99) | collective-permute-done | bytes 295968 | tf_op jit(solution)/shard_map/ppermute | solution.py:38
  456.6 5.5 %collective-permute-done.106.refs_3_ = bf16[136,1088]{1,0:T(8,128)(2,1)S(1)} collective-permute-done((bf16[136,1088]{1,0:T(8,128)(2,1)S(1)}, bf16[136,1088]{1,0:T(8,128)(2,1)S(1)}, u32[]{:S(2)}, u32[]{:S(2)}) %collective-permute-start.106) | collective-permute-done | bytes 295968 | tf_op jit(solution)/shard_map/ppermute | solution.py:38
  465.6 3.3 collective-permute-done.108.refs_5_
  474.6 4.1 lay_qkv.1
  480.2 4.3 lay_rows.4
  484.5 4.3 lay_rows.5
  488.7 2.6 lay_rows.3
  (490 shorter events, 177.2 us)
Async XLA Ops:
  5.6 25.9 %collective-permute-start.4 = (bf16[2176]{0:T(1024)(128)(2,1)S(1)}, bf16[2176]{0:T(1024)(128)(2,1)S(1)}, u32[]{:S(2)}, u32[]{:S(2)}) collective-permute-start(bf16[2176]{0:T(1024)(128)(2,1)S(1)} %concatenate.49), channel_id=1, source_target_pairs={{0,2},{1,3},{2,0},{3,1},{4,6},{5,7},{6,4},{7,5},{8,10},{9,11},{10,... | collective-permute-start | bytes 13064 | tf_op jit(solution)/shard_map/ppermute | solution.py:38
  8.7 23.9 %collective-permute-start.3 = (bf16[2176]{0:T(1024)(128)(2,1)S(1)}, bf16[2176]{0:T(1024)(128)(2,1)S(1)}, u32[]{:S(2)}, u32[]{:S(2)}) collective-permute-start(bf16[2176]{0:T(1024)(128)(2,1)S(1)} %concatenate.49), channel_id=1, source_target_pairs={{0,1},{1,0},{2,3},{3,2},{4,5},{5,4},{6,7},{7,6},{8,9},{9,8},{10,11... | collective-permute-start | bytes 13064 | tf_op jit(solution)/shard_map/ppermute | solution.py:38
  9.8 24.8 %collective-permute-start.6 = (bf16[128,1088]{1,0:T(8,128)(2,1)S(1)}, bf16[128,1088]{1,0:T(8,128)(2,1)S(1)}, u32[]{:S(2)}, u32[]{:S(2)}) collective-permute-start(bf16[128,1088]{1,0:T(8,128)(2,1)S(1)} %bitcast.129), channel_id=1, source_target_pairs={{0,4},{4,0},{8,12},{12,8},{16,20},{20,16},{24,28},{28,24},{1,5},{5... | collective-permute-start | bytes 835592 | tf_op jit(solution)/shard_map/ppermute | solution.py:38
  11.4 23.4 %collective-permute-start.7 = (bf16[128,1088]{1,0:T(8,128)(2,1)S(1)}, bf16[128,1088]{1,0:T(8,128)(2,1)}, u32[]{:S(2)}, u32[]{:S(2)}) collective-permute-start(bf16[128,1088]{1,0:T(8,128)(2,1)S(1)} %bitcast.130), channel_id=1, source_target_pairs={{0,8},{4,12},{8,0},{12,4},{16,24},{20,28},{24,16},{28,20},{1,9},{5... | collective-permute-start | bytes 835592 | tf_op jit(solution)/shard_map/ppermute | solution.py:38
  28.8 21.2 %collective-permute-start.9 = (bf16[128,1088]{1,0:T(8,128)(2,1)S(1)}, bf16[128,1088]{1,0:T(8,128)(2,1)}, u32[]{:S(2)}, u32[]{:S(2)}) collective-permute-start(bf16[128,1088]{1,0:T(8,128)(2,1)S(1)} %bitcast.131), channel_id=1, source_target_pairs={{0,16},{4,20},{8,24},{12,28},{16,0},{20,4},{24,8},{28,12},{1,17},{... | collective-permute-start | bytes 835592 | tf_op jit(solution)/shard_map/ppermute | solution.py:38
  32.6 18.8 %collective-permute-start.11 = (bf16[128,1088]{1,0:T(8,128)(2,1)S(1)}, bf16[128,1088]{1,0:T(8,128)(2,1)}, u32[]{:S(2)}, u32[]{:S(2)}) collective-permute-start(bf16[128,1088]{1,0:T(8,128)(2,1)S(1)} %bitcast.132), channel_id=1, source_target_pairs={{0,24},{4,28},{8,16},{12,20},{16,8},{20,12},{24,0},{28,4},{1,25},{... | collective-permute-start | bytes 835592 | tf_op jit(solution)/shard_map/ppermute | solution.py:38
  34.8 18.7 %collective-permute-start.8 = (bf16[128,1088]{1,0:T(8,128)(2,1)}, bf16[128,1088]{1,0:T(8,128)(2,1)}, u32[]{:S(2)}, u32[]{:S(2)}) collective-permute-start(bf16[128,1088]{1,0:T(8,128)(2,1)} %collective-permute-done.7.refs_2_), channel_id=1, source_target_pairs={{0,4},{4,0},{8,12},{12,8},{16,20},{20,16},{24,28},{28,24},{1,5},{5... | collective-permute-start | bytes 835592 | tf_op jit(solution)/shard_map/ppermute | solution.py:38
  50.0 35.0 %collective-permute-start.24 = (bf16[272,1088]{1,0:T(8,128)(2,1)S(1)}, bf16[272,1088]{1,0:T(8,128)(2,1)S(1)}, u32[]{:S(2)}, u32[]{:S(2)}) collective-permute-start(bf16[272,1088]{1,0:T(8,128)(2,1)S(1)} %copy-done.12), channel_id=1, source_target_pairs={{0,2},{1,3},{2,0},{3,1},{4,6},{5,7},{6,4},{7,5},{8,10},{9,11},{10,... | collective-permute-start | bytes 1775624 | tf_op jit(solution)/shard_map/ppermute | solution.py:38
  51.4 33.7 %collective-permute-start.23 = (bf16[272,1088]{1,0:T(8,128)(2,1)S(1)}, bf16[272,1088]{1,0:T(8,128)(2,1)S(1)}, u32[]{:S(2)}, u32[]{:S(2)}) collective-permute-start(bf16[272,1088]{1,0:T(8,128)(2,1)S(1)} %copy-done.12), channel_id=1, source_target_pairs={{0,1},{1,0},{2,3},{3,2},{4,5},{5,4},{6,7},{7,6},{8,9},{9,8},{10,11... | collective-permute-start | bytes 1775624 | tf_op jit(solution)/shard_map/ppermute | solution.py:38
  107.6 17.3 %collective-permute-start.32 = (bf16[128,1088]{1,0:T(8,128)(2,1)}, bf16[128,1088]{1,0:T(8,128)(2,1)S(1)}, u32[]{:S(2)}, u32[]{:S(2)}) collective-permute-start(bf16[128,1088]{1,0:T(8,128)(2,1)} %collective-permute-done.31.refs_2_), channel_id=1, source_target_pairs={{0,1},{1,0},{2,3},{3,2},{4,5},{5,4},{6,7},{7,6},{8,9},{9,8},{10,11... | collective-permute-start | bytes 835592 | tf_op jit(solution)/shard_map/ppermute | solution.py:38
  124.3 35.1 %collective-permute-start.28 = (bf16[128,1088]{1,0:T(8,128)(2,1)}, bf16[128,1088]{1,0:T(8,128)(2,1)S(1)}, u32[]{:S(2)}, u32[]{:S(2)}) collective-permute-start(bf16[128,1088]{1,0:T(8,128)(2,1)} %get-tuple-element.84), channel_id=1, source_target_pairs={{0,1},{1,0},{2,3},{3,2},{4,5},{5,4},{6,7},{7,6},{8,9},{9,8},{10,11... | collective-permute-start | bytes 835592 | tf_op jit(solution)/shard_map/ppermute | solution.py:38
  124.8 45.2 %collective-permute-start.35 = (bf16[128,1088]{1,0:T(8,128)(2,1)}, bf16[128,1088]{1,0:T(8,128)(2,1)S(1)}, u32[]{:S(2)}, u32[]{:S(2)}) collective-permute-start(bf16[128,1088]{1,0:T(8,128)(2,1)} %get-tuple-element.91), channel_id=1, source_target_pairs={{0,1},{1,0},{2,3},{3,2},{4,5},{5,4},{6,7},{7,6},{8,9},{9,8},{10,11... | collective-permute-start | bytes 835592 | tf_op jit(solution)/shard_map/ppermute | solution.py:38
  135.0 22.1 %collective-permute-start.33 = (bf16[128,1088]{1,0:T(8,128)(2,1)}, bf16[128,1088]{1,0:T(8,128)(2,1)S(1)}, u32[]{:S(2)}, u32[]{:S(2)}) collective-permute-start(bf16[128,1088]{1,0:T(8,128)(2,1)} %get-tuple-element.86), channel_id=1, source_target_pairs={{0,1},{1,0},{2,3},{3,2},{4,5},{5,4},{6,7},{7,6},{8,9},{9,8},{10,11... | collective-permute-start | bytes 835592 | tf_op jit(solution)/shard_map/ppermute | solution.py:38
  135.5 23.3 %collective-permute-start.36 = (bf16[128,1088]{1,0:T(8,128)(2,1)}, bf16[128,1088]{1,0:T(8,128)(2,1)S(1)}, u32[]{:S(2)}, u32[]{:S(2)}) collective-permute-start(bf16[128,1088]{1,0:T(8,128)(2,1)} %get-tuple-element.93), channel_id=1, source_target_pairs={{0,1},{1,0},{2,3},{3,2},{4,5},{5,4},{6,7},{7,6},{8,9},{9,8},{10,11... | collective-permute-start | bytes 835592 | tf_op jit(solution)/shard_map/ppermute | solution.py:38
  202.9 78.5 %collective-permute-start.52 = (bf16[816,1088]{1,0:T(8,128)(2,1)S(1)}, bf16[816,1088]{1,0:T(8,128)(2,1)}, u32[]{:S(2)}, u32[]{:S(2)}) collective-permute-start(bf16[816,1088]{1,0:T(8,128)(2,1)S(1)} %pad_maximum_fusion.refs_8_), channel_id=1, source_target_pairs={{0,1},{1,0},{2,3},{3,2},{4,5},{5,4},{6,7},{7,6},{8,9},{9,8},{10,11... | collective-permute-start | bytes 5326856 | tf_op jit(solution)/shard_map/ppermute | solution.py:38
  203.0 43.5 %collective-permute-start.53 = (bf16[816,1088]{1,0:T(8,128)(2,1)S(1)}, bf16[816,1088]{1,0:T(8,128)(2,1)}, u32[]{:S(2)}, u32[]{:S(2)}) collective-permute-start(bf16[816,1088]{1,0:T(8,128)(2,1)S(1)} %pad_maximum_fusion.refs_8_), channel_id=1, source_target_pairs={{0,2},{1,3},{2,0},{3,1},{4,6},{5,7},{6,4},{7,5},{8,10},{9,11},{10,... | collective-permute-start | bytes 5326856 | tf_op jit(solution)/shard_map/ppermute | solution.py:38
  204.6 47.7 %collective-permute-start.89 = (bf16[4,136,1088]{2,1,0:T(8,128)(2,1)}, bf16[4,136,1088]{2,1,0:T(8,128)(2,1)S(1)}, u32[]{:S(2)}, u32[]{:S(2)}) collective-permute-start(bf16[4,136,1088]{2,1,0:T(8,128)(2,1)} %fusion), channel_id=1, source_target_pairs={{0,4},{4,0},{8,12},{12,8},{16,20},{20,16},{24,28},{28,24},{1,5},{5... | collective-permute-start | bytes 3551240 | tf_op jit(solution)/shard_map/ppermute | solution.py:38
  205.6 43.1 %collective-permute-start.71 = (bf16[272,1088]{1,0:T(8,128)(2,1)}, bf16[272,1088]{1,0:T(8,128)(2,1)}, u32[]{:S(2)}, u32[]{:S(2)}) collective-permute-start(bf16[272,1088]{1,0:T(8,128)(2,1)} %get-tuple-element.184), channel_id=1, source_target_pairs={{0,1},{1,0},{2,3},{3,2},{4,5},{5,4},{6,7},{7,6},{8,9},{9,8},{10,11... | collective-permute-start | bytes 1775624 | tf_op jit(solution)/shard_map/ppermute | solution.py:38
  205.6 24.2 %collective-permute-start.87 = (f32[1,4352]{1,0:T(1,128)}, f32[1,4352]{1,0:T(1,128)}, u32[]{:S(2)}, u32[]{:S(2)}) collective-permute-start(f32[1,4352]{1,0:T(1,128)} %slice.160), channel_id=1, source_target_pairs={{0,1},{1,0},{2,3},{3,2},{4,5},{5,4},{6,7},{7,6},{8,9},{9,8},{10,11... | collective-permute-start | bytes 52232 | tf_op jit(solution)/shard_map/ppermute | solution.py:38
  229.8 17.7 %collective-permute-start.61 = (bf16[272,768]{1,0:T(8,128)(2,1)}, bf16[272,768]{1,0:T(8,128)(2,1)S(1)}, u32[]{:S(2)}, u32[]{:S(2)}) collective-permute-start(bf16[272,768]{1,0:T(8,128)(2,1)} %get-tuple-element.186), channel_id=1, source_target_pairs={{0,1},{1,0},{2,3},{3,2},{4,5},{5,4},{6,7},{7,6},{8,9},{9,8},{10,11... | collective-permute-start | bytes 1253384 | tf_op jit(solution)/shard_map/ppermute | solution.py:38
  246.5 30.4 %collective-permute-start.100 = (bf16[4,136,1088]{2,1,0:T(8,128)(2,1)}, bf16[4,136,1088]{2,1,0:T(8,128)(2,1)S(1)}, u32[]{:S(2)}, u32[]{:S(2)}) collective-permute-start(bf16[4,136,1088]{2,1,0:T(8,128)(2,1)} %fusion.1), channel_id=1, source_target_pairs={{0,4},{4,0},{8,12},{12,8},{16,20},{20,16},{24,28},{28,24},{1,5},{5... | collective-permute-start | bytes 3551240 | tf_op jit(solution)/shard_map/ppermute | solution.py:38
  247.4 69.8 %collective-permute-start.54 = (bf16[816,1088]{1,0:T(8,128)(2,1)}, bf16[816,1088]{1,0:T(8,128)(2,1)S(1)}, u32[]{:S(2)}, u32[]{:S(2)}) collective-permute-start(bf16[816,1088]{1,0:T(8,128)(2,1)} %collective-permute-done.53.refs_10_), channel_id=1, source_target_pairs={{0,1},{1,0},{2,3},{3,2},{4,5},{5,4},{6,7},{7,6},{8,9},{9,8},{10,11... | collective-permute-start | bytes 5326856 | tf_op jit(solution)/shard_map/ppermute | solution.py:38
  248.7 32.9 %collective-permute-start.45 = (bf16[128,384]{1,0:T(8,128)(2,1)}, bf16[128,384]{1,0:T(8,128)(2,1)S(1)}, u32[]{:S(2)}, u32[]{:S(2)}) collective-permute-start(bf16[128,384]{1,0:T(8,128)(2,1)} %get-tuple-element.105), channel_id=1, source_target_pairs={{0,4},{4,0},{8,12},{12,8},{16,20},{20,16},{24,28},{28,24},{1,5},{5... | collective-permute-start | bytes 294920 | tf_op jit(solution)/shard_map/ppermute | solution.py:38
  252.3 37.8 %collective-permute-start.60 = (bf16[272,768]{1,0:T(8,128)(2,1)S(1)}, bf16[272,768]{1,0:T(8,128)(2,1)S(1)}, u32[]{:S(2)}, u32[]{:S(2)}) collective-permute-start(bf16[272,768]{1,0:T(8,128)(2,1)S(1)} %get-tuple-element.185), channel_id=1, source_target_pairs={{0,1},{1,0},{2,3},{3,2},{4,5},{5,4},{6,7},{7,6},{8,9},{9,8},{10,11... | collective-permute-start | bytes 1253384 | tf_op jit(solution)/shard_map/ppermute | solution.py:38
  297.5 49.1 %collective-permute-start.70 = (bf16[272,1088]{1,0:T(8,128)(2,1)S(1)}, bf16[272,1088]{1,0:T(8,128)(2,1)S(1)}, u32[]{:S(2)}, u32[]{:S(2)}) collective-permute-start(bf16[272,1088]{1,0:T(8,128)(2,1)S(1)} %copy-done.20), channel_id=1, source_target_pairs={{0,1},{1,0},{2,3},{3,2},{4,5},{5,4},{6,7},{7,6},{8,9},{9,8},{10,11... | collective-permute-start | bytes 1775624 | tf_op jit(solution)/shard_map/ppermute | solution.py:38
  301.0 30.6 %collective-permute-start.92 = (bf16[136,1088]{1,0:T(8,128)(2,1)}, bf16[136,1088]{1,0:T(8,128)(2,1)S(1)}, u32[]{:S(2)}, u32[]{:S(2)}) collective-permute-start(bf16[136,1088]{1,0:T(8,128)(2,1)} %get-tuple-element.191), channel_id=1, source_target_pairs={{0,24},{4,28},{8,16},{12,20},{16,8},{20,12},{24,0},{28,4},{1,25},{... | collective-permute-start | bytes 887816 | tf_op jit(solution)/shard_map/ppermute | solution.py:38
  303.2 30.1 %collective-permute-start.91 = (bf16[136,1088]{1,0:T(8,128)(2,1)}, bf16[136,1088]{1,0:T(8,128)(2,1)S(1)}, u32[]{:S(2)}, u32[]{:S(2)}) collective-permute-start(bf16[136,1088]{1,0:T(8,128)(2,1)} %get-tuple-element.192), channel_id=1, source_target_pairs={{0,16},{4,20},{8,24},{12,28},{16,0},{20,4},{24,8},{28,12},{1,17},{... | collective-permute-start | bytes 887816 | tf_op jit(solution)/shard_map/ppermute | solution.py:38
  305.9 30.4 %collective-permute-start.90 = (bf16[136,1088]{1,0:T(8,128)(2,1)}, bf16[136,1088]{1,0:T(8,128)(2,1)}, u32[]{:S(2)}, u32[]{:S(2)}) collective-permute-start(bf16[136,1088]{1,0:T(8,128)(2,1)} %get-tuple-element.190), channel_id=1, source_target_pairs={{0,8},{4,12},{8,0},{12,4},{16,24},{20,28},{24,16},{28,20},{1,9},{5... | collective-permute-start | bytes 887816 | tf_op jit(solution)/shard_map/ppermute | solution.py:38
  331.7 27.9 %collective-permute-start.88 = (f32[1,4352]{1,0:T(1,128)S(1)}, f32[1,4352]{1,0:T(1,128)S(1)}, u32[]{:S(2)}, u32[]{:S(2)}) collective-permute-start(f32[1,4352]{1,0:T(1,128)S(1)} %copy-done.61), channel_id=1, source_target_pairs={{0,2},{1,3},{2,0},{3,1},{4,6},{5,7},{6,4},{7,5},{8,10},{9,11},{10,... | collective-permute-start | bytes 52232 | tf_op jit(solution)/shard_map/ppermute | solution.py:38
  334.0 25.6 %collective-permute-start.103 = (bf16[136,1088]{1,0:T(8,128)(2,1)}, bf16[136,1088]{1,0:T(8,128)(2,1)S(1)}, u32[]{:S(2)}, u32[]{:S(2)}) collective-permute-start(bf16[136,1088]{1,0:T(8,128)(2,1)} %get-tuple-element.188), channel_id=1, source_target_pairs={{0,24},{4,28},{8,16},{12,20},{16,8},{20,12},{24,0},{28,4},{1,25},{... | collective-permute-start | bytes 887816 | tf_op jit(solution)/shard_map/ppermute | solution.py:38
  344.4 17.4 %collective-permute-start.102 = (bf16[136,1088]{1,0:T(8,128)(2,1)}, bf16[136,1088]{1,0:T(8,128)(2,1)S(1)}, u32[]{:S(2)}, u32[]{:S(2)}) collective-permute-start(bf16[136,1088]{1,0:T(8,128)(2,1)} %get-tuple-element.189), channel_id=1, source_target_pairs={{0,16},{4,20},{8,24},{12,28},{16,0},{20,4},{24,8},{28,12},{1,17},{... | collective-permute-start | bytes 887816 | tf_op jit(solution)/shard_map/ppermute | solution.py:38
  375.7 25.6 %collective-permute-start.96 = (bf16[136,1088]{1,0:T(8,128)(2,1)S(1)}, bf16[136,1088]{1,0:T(8,128)(2,1)S(1)}, u32[]{:S(2)}, u32[]{:S(2)}) collective-permute-start(bf16[136,1088]{1,0:T(8,128)(2,1)S(1)} %fusion.36.refs_0_), channel_id=1, source_target_pairs={{0,16},{4,20},{8,24},{12,28},{16,0},{20,4},{24,8},{28,12},{1,17},{... | collective-permute-start | bytes 887816 | tf_op jit(solution)/shard_map/ppermute | solution.py:38
  375.7 25.6 %collective-permute-start.73 = (bf16[4,48,1088]{2,1,0:T(8,128)(2,1)S(1)}, bf16[4,48,1088]{2,1,0:T(8,128)(2,1)S(1)}, u32[]{:S(2)}, u32[]{:S(2)}) collective-permute-start(bf16[4,48,1088]{2,1,0:T(8,128)(2,1)S(1)} %fusion.37), channel_id=1, source_target_pairs={{0,4},{4,0},{8,12},{12,8},{16,20},{20,16},{24,28},{28,24},{1,5},{5... | collective-permute-start | bytes 1253384 | tf_op jit(solution)/shard_map/ppermute | solution.py:38
  378.5 24.3 %collective-permute-start.98 = (bf16[136,1088]{1,0:T(8,128)(2,1)S(1)}, bf16[136,1088]{1,0:T(8,128)(2,1)S(1)}, u32[]{:S(2)}, u32[]{:S(2)}) collective-permute-start(bf16[136,1088]{1,0:T(8,128)(2,1)S(1)} %fusion.36.refs_0_), channel_id=1, source_target_pairs={{0,24},{4,28},{8,16},{12,20},{16,8},{20,12},{24,0},{28,4},{1,25},{... | collective-permute-start | bytes 887816 | tf_op jit(solution)/shard_map/ppermute | solution.py:38
  380.5 24.3 %collective-permute-start.104 = (bf16[136,1088]{1,0:T(8,128)(2,1)S(1)}, bf16[136,1088]{1,0:T(8,128)(2,1)S(1)}, u32[]{:S(2)}, u32[]{:S(2)}) collective-permute-start(bf16[136,1088]{1,0:T(8,128)(2,1)S(1)} %fusion.33.refs_0_), channel_id=1, source_target_pairs={{0,4},{4,0},{8,12},{12,8},{16,20},{20,16},{24,28},{28,24},{1,5},{5... | collective-permute-start | bytes 887816 | tf_op jit(solution)/shard_map/ppermute | solution.py:38
  381.3 23.7 %collective-permute-start.105 = (bf16[136,1088]{1,0:T(8,128)(2,1)S(1)}, bf16[136,1088]{1,0:T(8,128)(2,1)S(1)}, u32[]{:S(2)}, u32[]{:S(2)}) collective-permute-start(bf16[136,1088]{1,0:T(8,128)(2,1)S(1)} %fusion.33.refs_0_), channel_id=1, source_target_pairs={{0,8},{4,12},{8,0},{12,4},{16,24},{20,28},{24,16},{28,20},{1,9},{5... | collective-permute-start | bytes 887816 | tf_op jit(solution)/shard_map/ppermute | solution.py:38
  401.4 25.8 %collective-permute-start.107 = (bf16[136,1088]{1,0:T(8,128)(2,1)S(1)}, bf16[136,1088]{1,0:T(8,128)(2,1)S(1)}, u32[]{:S(2)}, u32[]{:S(2)}) collective-permute-start(bf16[136,1088]{1,0:T(8,128)(2,1)S(1)} %fusion.33.refs_0_), channel_id=1, source_target_pairs={{0,16},{4,20},{8,24},{12,28},{16,0},{20,4},{24,8},{28,12},{1,17},{... | collective-permute-start | bytes 887816 | tf_op jit(solution)/shard_map/ppermute | solution.py:38
  401.4 27.3 %collective-permute-start.109 = (bf16[136,1088]{1,0:T(8,128)(2,1)S(1)}, bf16[136,1088]{1,0:T(8,128)(2,1)}, u32[]{:S(2)}, u32[]{:S(2)}) collective-permute-start(bf16[136,1088]{1,0:T(8,128)(2,1)S(1)} %fusion.33.refs_0_), channel_id=1, source_target_pairs={{0,24},{4,28},{8,16},{12,20},{16,8},{20,12},{24,0},{28,4},{1,25},{... | collective-permute-start | bytes 887816 | tf_op jit(solution)/shard_map/ppermute | solution.py:38
  402.9 26.4 %collective-permute-start.65 = (bf16[272,384]{1,0:T(8,128)(2,1)S(1)}, bf16[272,384]{1,0:T(8,128)(2,1)S(1)}, u32[]{:S(2)}, u32[]{:S(2)}) collective-permute-start(bf16[272,384]{1,0:T(8,128)(2,1)S(1)} %collective-permute-done.64.refs_2_), channel_id=1, source_target_pairs={{0,4},{4,0},{8,12},{12,8},{16,20},{20,16},{24,28},{28,24},{1,5},{5... | collective-permute-start | bytes 626696 | tf_op jit(solution)/shard_map/ppermute | solution.py:38
  404.9 26.2 %collective-permute-start.67 = (bf16[272,384]{1,0:T(8,128)(2,1)S(1)}, bf16[272,384]{1,0:T(8,128)(2,1)S(1)}, u32[]{:S(2)}, u32[]{:S(2)}) collective-permute-start(bf16[272,384]{1,0:T(8,128)(2,1)S(1)} %collective-permute-done.66.refs_4_), channel_id=1, source_target_pairs={{0,4},{4,0},{8,12},{12,8},{16,20},{20,16},{24,28},{28,24},{1,5},{5... | collective-permute-start | bytes 626696 | tf_op jit(solution)/shard_map/ppermute | solution.py:38
  405.0 31.1 %collective-permute-start.69 = (bf16[272,384]{1,0:T(8,128)(2,1)S(1)}, bf16[272,384]{1,0:T(8,128)(2,1)S(1)}, u32[]{:S(2)}, u32[]{:S(2)}) collective-permute-start(bf16[272,384]{1,0:T(8,128)(2,1)S(1)} %collective-permute-done.68.refs_6_), channel_id=1, source_target_pairs={{0,4},{4,0},{8,12},{12,8},{16,20},{20,16},{24,28},{28,24},{1,5},{5... | collective-permute-start | bytes 626696 | tf_op jit(solution)/shard_map/ppermute | solution.py:38
  440.5 21.7 %collective-permute-start.106 = (bf16[136,1088]{1,0:T(8,128)(2,1)S(1)}, bf16[136,1088]{1,0:T(8,128)(2,1)S(1)}, u32[]{:S(2)}, u32[]{:S(2)}) collective-permute-start(bf16[136,1088]{1,0:T(8,128)(2,1)S(1)} %collective-permute-done.105.refs_2_), channel_id=1, source_target_pairs={{0,4},{4,0},{8,12},{12,8},{16,20},{20,16},{24,28},{28,24},{1,5},{5... | collective-permute-start | bytes 887816 | tf_op jit(solution)/shard_map/ppermute | solution.py:38
  442.9 26.0 %collective-permute-start.108 = (bf16[136,1088]{1,0:T(8,128)(2,1)S(1)}, bf16[136,1088]{1,0:T(8,128)(2,1)S(1)}, u32[]{:S(2)}, u32[]{:S(2)}) collective-permute-start(bf16[136,1088]{1,0:T(8,128)(2,1)S(1)} %collective-permute-done.107.refs_4_), channel_id=1, source_target_pairs={{0,4},{4,0},{8,12},{12,8},{16,20},{20,16},{24,28},{28,24},{1,5},{5... | collective-permute-start | bytes 887816 | tf_op jit(solution)/shard_map/ppermute | solution.py:38
  443.6 40.9 %collective-permute-start.110 = (bf16[136,1088]{1,0:T(8,128)(2,1)}, bf16[136,1088]{1,0:T(8,128)(2,1)}, u32[]{:S(2)}, u32[]{:S(2)}) collective-permute-start(bf16[136,1088]{1,0:T(8,128)(2,1)} %collective-permute-done.109.refs_6_), channel_id=1, source_target_pairs={{0,4},{4,0},{8,12},{12,8},{16,20},{20,16},{24,28},{28,24},{1,5},{5... | collective-permute-start | bytes 887816 | tf_op jit(solution)/shard_map/ppermute | solution.py:38
  448.8 21.1 %collective-permute-start.78 = (bf16[48,1088]{1,0:T(8,128)(2,1)S(1)}, bf16[48,1088]{1,0:T(8,128)(2,1)S(1)}, u32[]{:S(2)}, u32[]{:S(2)}) collective-permute-start(bf16[48,1088]{1,0:T(8,128)(2,1)S(1)} %fusion.48.refs_0_), channel_id=1, source_target_pairs={{0,8},{4,12},{8,0},{12,4},{16,24},{20,28},{24,16},{28,20},{1,9},{5... | collective-permute-start | bytes 313352 | tf_op jit(solution)/shard_map/ppermute | solution.py:38
  468.9 19.8 %collective-permute-start.77 = (bf16[48,1088]{1,0:T(8,128)(2,1)S(1)}, bf16[48,1088]{1,0:T(8,128)(2,1)}, u32[]{:S(2)}, u32[]{:S(2)}) collective-permute-start(bf16[48,1088]{1,0:T(8,128)(2,1)S(1)} %fusion.48.refs_0_), channel_id=1, source_target_pairs={{0,4},{4,0},{8,12},{12,8},{16,20},{20,16},{24,28},{28,24},{1,5},{5... | collective-permute-start | bytes 313352 | tf_op jit(solution)/shard_map/ppermute | solution.py:38
  469.8 18.9 %collective-permute-start.79 = (bf16[48,1088]{1,0:T(8,128)(2,1)S(1)}, bf16[48,1088]{1,0:T(8,128)(2,1)}, u32[]{:S(2)}, u32[]{:S(2)}) collective-permute-start(bf16[48,1088]{1,0:T(8,128)(2,1)S(1)} %collective-permute-done.78.refs_2_), channel_id=1, source_target_pairs={{0,4},{4,0},{8,12},{12,8},{16,20},{20,16},{24,28},{28,24},{1,5},{5... | collective-permute-start | bytes 313352 | tf_op jit(solution)/shard_map/ppermute | solution.py:38
  470.9 17.8 %collective-permute-start.81 = (bf16[48,1088]{1,0:T(8,128)(2,1)S(1)}, bf16[48,1088]{1,0:T(8,128)(2,1)}, u32[]{:S(2)}, u32[]{:S(2)}) collective-permute-start(bf16[48,1088]{1,0:T(8,128)(2,1)S(1)} %collective-permute-done.80.refs_4_), channel_id=1, source_target_pairs={{0,4},{4,0},{8,12},{12,8},{16,20},{20,16},{24,28},{28,24},{1,5},{5... | collective-permute-start | bytes 313352 | tf_op jit(solution)/shard_map/ppermute | solution.py:38
  (161 other events, 2968.2 us)
